TPU v7x, 128 devices: a whole 4x4x4 slice. The times are simulated.
128 devices in a mesh: dp: 8 (over z, x_lo), frame: 16 (over y, x_hi, core).
Axes of the slice: x: 4 (x_hi: 2, x_lo: 2; x = x_hi * 2 + x_lo), y: 4, z: 4, core: 2. Of those that a mesh axis runs over, the one named last changes fastest.
Arguments:
- latents: bfloat16 [128, 1024, 256], P(('dp', 'frame')), parts along dimension 0, may hold values from -6 to 6
- cotangent: bfloat16 [128, 1024, 256], P(('dp', 'frame')), parts along dimension 0, may hold values from -6 to 6
- gain_time: float32 [256], replicated, may hold values from 0.5 to 1.5
- qkv_time: bfloat16 [256, 768], replicated, may hold values from -3 to 3, as said below
- out_time: bfloat16 [256, 256], replicated, may hold values from -0.375 to 0.375
- gain_space: float32 [256], replicated, may hold values from 0.5 to 1.5
- qkv_space: bfloat16 [256, 768], replicated, may hold values from -3 to 3, as said below
- out_space: bfloat16 [256, 256], replicated, may hold values from -0.375 to 0.375
Outputs:
- grad_latents: float32 [128, 1024, 256], P(('dp', 'frame')), parts along dimension 0
- grad_qkv_time: float32 [2048, 768], P(('dp', 'frame')), parts along dimension 0
- grad_out_time: float32 [2048, 256], P(('dp', 'frame')), parts along dimension 0
- grad_qkv_space: float32 [2048, 768], P(('dp', 'frame')), parts along dimension 0
- grad_out_space: float32 [2048, 256], P(('dp', 'frame')), parts along dimension 0
- grad_gain_time: float32 [2048], P(('dp', 'frame')), parts along dimension 0
- grad_gain_space: float32 [2048], P(('dp', 'frame')), parts along dimension 0
There are 8 independent parts, one for each index of `dp`. A program takes and returns all parts, laid end to end along the dimension named above; an argument that names none is the same for every part. Nothing has to cross between parts.
Inputs may be any that keep to these rules, and one draw needn't show every extreme that they name: `qkv_time`: entries of a projection scaled by fan-in. `qkv_space`: entries of a projection scaled by fan-in.
All inputs are finite; a program needn't handle non-finite values.
Results may differ from a plain program's by a relative error of at most 0.035.
Values may be sent and summed in bfloat16 or wider, within the bound.
No kernel may reach another device: no remote copies, remote signals or barrier semaphores. Data moves between devices by JAX's collectives and lax.ppermute only.
A program may use at most 128 MiB of HBM per device.

v0:
```python
import functools

import jax
import jax.numpy as jnp
from jax import lax
from jax.experimental import pallas as pl
from jax.experimental.pallas import tpu as pltpu
from jax.sharding import PartitionSpec as P

HEADS = 8
HEAD_DIM = 32
D = 256
WIN = 8
HH = 32
WW = 32
FRAMES = 16
TOKENS = 1024
ROWS = 1024
SHARE = 64
GROUP = 128
HALF = 128
PACK = 4
CHUNK = 256
EPSILON = 1e-06
SCALE = HEAD_DIM ** (-0.5)
MASKED = -1e30
F32 = jnp.float32
BF16 = jnp.bfloat16


def dot_nn(a, b):
    return lax.dot_general(a, b, (((1,), (0,)), ((), ())), preferred_element_type=F32)


def dot_nt(a, b):
    return lax.dot_general(a, b, (((1,), (1,)), ((), ())), preferred_element_type=F32)


def dot_tn(a, b):
    return lax.dot_general(a, b, (((0,), (0,)), ((), ())), preferred_element_type=F32)


def head_masks():
    lane = lax.broadcasted_iota(jnp.int32, (1, HALF), 1) // HEAD_DIM
    return [(lane == h).astype(F32).astype(BF16) for h in range(PACK)]


def spread(x, masks):
    return jnp.concatenate([x * m for m in masks], axis=0)


def flip(x):
    return jnp.concatenate([x[:, GROUP * h : GROUP * (h + 1)].T for h in range(PACK)], axis=1)


def soft_probs(q, k, masks, bias):
    qb = spread(q, masks)
    scores = dot_nt(k, qb) * SCALE + bias
    top = jnp.max(scores, axis=0, keepdims=True)
    ex = jnp.exp(scores - top)
    return ex * (1.0 / jnp.sum(ex, axis=0, keepdims=True)), qb


def mix(probs, v, masks):
    return dot_nn(flip(probs), spread(v, masks)).astype(BF16)


def attend_back(q, k, v, do, probs, qb, masks):
    dob = spread(do, masks)
    dv = dot_nn(probs.astype(BF16), dob)
    dp = dot_nt(v, dob)
    weighted = probs.astype(F32) * dp
    inner = jnp.sum(weighted, axis=0, keepdims=True)
    ds = (weighted - probs.astype(F32) * inner).astype(BF16)
    dk = dot_nn(ds, qb) * SCALE
    dq = dot_nn(flip(ds), spread(k, masks)) * SCALE
    return dq.astype(BF16), dk.astype(BF16), dv.astype(BF16)


def norm_factor(x):
    return lax.rsqrt(jnp.mean(x * x, -1, keepdims=True) + EPSILON)


def main_kernel(
    moved, gain_t, qkv_t, out_t, gain_s, qkv_s, out_s, sent,
    xs, cots, proj_t, probs_t, mixed_t, middle, proj_s, mixed_s, dmix, dproj, dmid, grads, in_t, in_s,
):
    masks = head_masks()
    row = lax.broadcasted_iota(jnp.int32, (GROUP, PACK * GROUP), 0)
    col = lax.broadcasted_iota(jnp.int32, (GROUP, PACK * GROUP), 1)
    bias_t = jnp.where(row % WIN == col % WIN, 0.0, MASKED).astype(F32)
    bias_s = jnp.where((row // WIN) % 2 == (col // WIN) % 2, 0.0, MASKED).astype(F32)

    def reorder(f, _):
        for p in range(SHARE // 16):
            for src, dst, base in ((moved, xs, 0), (moved, cots, SHARE)):
                both = src[f, base + 16 * p : base + 16 * (p + 1), :].astype(F32)
                dst[pl.ds(pl.multiple_of(2 * p * GROUP + f * WIN, WIN), WIN), :] = both[:WIN]
                dst[pl.ds(pl.multiple_of((2 * p + 1) * GROUP + f * WIN, WIN), WIN), :] = both[WIN:]
        return _

    lax.fori_loop(0, FRAMES, reorder, 0)

    def rows_of(c):
        return pl.ds(pl.multiple_of(c * CHUNK, CHUNK), CHUNK)

    def pair_of(c):
        return pl.ds(2 * c, 2)

    def fold(x):
        return x.reshape(2, GROUP, x.shape[1])

    def project_time(c, _):
        x = xs[rows_of(c), :]
        inp = (x * norm_factor(x) * gain_t[...]).astype(BF16)
        in_t[rows_of(c), :] = inp
        proj_t[rows_of(c), :] = dot_nn(inp, qkv_t[...]).astype(BF16)
        return _

    lax.fori_loop(0, ROWS // CHUNK, project_time, 0)

    def time_forward(t, _):
        rows = pl.ds(pl.multiple_of(t * GROUP, GROUP), GROUP)
        for half in range(2):
            lanes = slice(HALF * half, HALF * (half + 1))
            q = proj_t[rows, lanes]
            k = proj_t[rows, D + HALF * half : D + HALF * (half + 1)]
            v = proj_t[rows, 2 * D + HALF * half : 2 * D + HALF * (half + 1)]
            probs, qb = soft_probs(q, k, masks, bias_t)
            probs = probs.astype(BF16)
            probs_t[2 * t + half] = probs
            mixed_t[rows, lanes] = mix(probs, v, masks)
        return _

    lax.fori_loop(0, ROWS // GROUP, time_forward, 0)

    def project_space(c, _):
        mid = (xs[rows_of(c), :] + dot_nn(mixed_t[rows_of(c), :], out_t[...])).astype(BF16)
        middle[rows_of(c), :] = mid
        mid = mid.astype(F32)
        inp = (mid * norm_factor(mid) * gain_s[...]).astype(BF16)
        in_s[rows_of(c), :] = inp
        proj_s[pair_of(c)] = fold(dot_nn(inp, qkv_s[...]).astype(BF16))
        dmix[pair_of(c)] = fold(dot_nt(cots[rows_of(c), :].astype(BF16), out_s[...]).astype(BF16))
        return _

    lax.fori_loop(0, ROWS // CHUNK, project_space, 0)

    def space(g, _):
        rows = pl.ds(pl.multiple_of(g * 16, 16), 16)

        def take(ref, first):
            return ref[:, rows, first : first + HALF].reshape(GROUP, HALF)

        def put(ref, first, x):
            ref[:, rows, first : first + HALF] = x.reshape(ROWS // GROUP, 16, HALF)

        for half in range(2):
            first = HALF * half
            q, k, v = (take(proj_s, D * i + first) for i in range(3))
            probs, qb = soft_probs(q, k, masks, bias_s)
            put(mixed_s, first, mix(probs.astype(BF16), v, masks))
            grad3 = attend_back(q, k, v, take(dmix, first), probs, qb, masks)
            for i in range(3):
                put(dproj, D * i + first, grad3[i])
        return _

    lax.fori_loop(0, FRAMES // 2, space, 0)

    def place(first, sums):
        sums = sums.astype(BF16)
        for d in range(FRAMES):
            sent[d, first : first + 16, :] = sums[16 * d : 16 * (d + 1), :]

    for i in range(3):
        place(128 + 16 * i, dot_tn(in_s[...], dproj[:, :, D * i : D * (i + 1)].reshape(ROWS, D)))
    place(128 + 48, dot_tn(mixed_s[...].reshape(ROWS, D), cots[...].astype(BF16)))

    def middle_back(c, gain_sum):
        dinput = dot_nt(dproj[pair_of(c)].reshape(CHUNK, 3 * D), qkv_s[...])
        mid = middle[rows_of(c), :].astype(F32)
        factor = norm_factor(mid)
        normed = mid * factor
        scaled = dinput * gain_s[...]
        dm = cots[rows_of(c), :] + factor * (
            scaled - normed * jnp.mean(scaled * normed, -1, keepdims=True)
        )
        dmid[rows_of(c), :] = dm
        dmix[pair_of(c)] = fold(dot_nt(dm.astype(BF16), out_t[...]).astype(BF16))
        return gain_sum + jnp.sum(dinput * normed, axis=0, keepdims=True)

    gain_sum_s = lax.fori_loop(0, ROWS // CHUNK, middle_back, jnp.zeros((1, D), F32))

    def time_back(t, _):
        rows = pl.ds(pl.multiple_of(t * GROUP, GROUP), GROUP)
        for half in range(2):
            first = HALF * half
            q, k, v = (proj_t[rows, D * i + first : D * i + first + HALF] for i in range(3))
            grad3 = attend_back(
                q, k, v, dmix[t, :, first : first + HALF], probs_t[2 * t + half], spread(q, masks), masks
            )
            for i in range(3):
                dproj[t, :, D * i + first : D * i + first + HALF] = grad3[i]
        return _

    lax.fori_loop(0, ROWS // GROUP, time_back, 0)

    for i in range(3):
        place(64 + 16 * i, dot_tn(in_t[...], dproj[:, :, D * i : D * (i + 1)].reshape(ROWS, D)))
    place(64 + 48, dot_tn(mixed_t[...], dmid[...].astype(BF16)))

    def input_back(c, gain_sum):
        dinput = dot_nt(dproj[pair_of(c)].reshape(CHUNK, 3 * D), qkv_t[...])
        x = xs[rows_of(c), :]
        factor = norm_factor(x)
        normed = x * factor
        scaled = dinput * gain_t[...]
        grads[rows_of(c), :] = dmid[rows_of(c), :] + factor * (
            scaled - normed * jnp.mean(scaled * normed, -1, keepdims=True)
        )
        return gain_sum + jnp.sum(dinput * normed, axis=0, keepdims=True)

    gain_sum_t = lax.fori_loop(0, ROWS // CHUNK, input_back, jnp.zeros((1, D), F32))

    gains = jnp.concatenate([gain_sum_t, gain_sum_s], axis=0)
    high = gains.astype(BF16).astype(F32)
    low = gains - high
    extra = jnp.concatenate([high, low, jnp.zeros((12, D), F32)], axis=0).astype(BF16)

    def restore(f, _):
        for p in range(SHARE // 16):
            first = grads[pl.ds(pl.multiple_of(2 * p * GROUP + f * WIN, WIN), WIN), :]
            second = grads[pl.ds(pl.multiple_of((2 * p + 1) * GROUP + f * WIN, WIN), WIN), :]
            sent[f, 16 * p : 16 * (p + 1), :] = jnp.concatenate([first, second], axis=0).astype(BF16)
        sent[f, 192:208, :] = extra
        return _

    lax.fori_loop(0, FRAMES, restore, 0)


def run_main(moved, gain_t, qkv_t, out_t, gain_s, qkv_s, out_s):
    return pl.pallas_call(
        main_kernel,
        out_shape=jax.ShapeDtypeStruct((FRAMES, 208, D), BF16),
        scratch_shapes=[
            pltpu.VMEM((ROWS, D), F32),
            pltpu.VMEM((ROWS, D), F32),
            pltpu.VMEM((ROWS, 3 * D), BF16),
            pltpu.VMEM((16, GROUP, PACK * GROUP), BF16),
            pltpu.VMEM((ROWS, D), BF16),
            pltpu.VMEM((ROWS, D), BF16),
            pltpu.VMEM((ROWS // GROUP, GROUP, 3 * D), BF16),
            pltpu.VMEM((ROWS // GROUP, GROUP, D), BF16),
            pltpu.VMEM((ROWS // GROUP, GROUP, D), BF16),
            pltpu.VMEM((ROWS // GROUP, GROUP, 3 * D), BF16),
            pltpu.VMEM((ROWS, D), F32),
            pltpu.VMEM((ROWS, D), F32),
            pltpu.VMEM((ROWS, D), BF16),
            pltpu.VMEM((ROWS, D), BF16),
        ],
        compiler_params=pltpu.CompilerParams(vmem_limit_bytes=40 * 1024 * 1024),
        cost_estimate=pl.CostEstimate(
            flops=8 * 10**9, bytes_accessed=6 * 10**6, transcendentals=2 * 10**6
        ),
    )(moved, gain_t.reshape(1, D), qkv_t, out_t, gain_s.reshape(1, D), qkv_s, out_s)


def to_windows(frame):
    split = frame.reshape(HH // WIN, WIN, WW // WIN, WIN, D)
    return split.transpose(0, 2, 1, 3, 4).reshape(FRAMES, SHARE, D)


def from_windows(windows):
    split = windows.reshape(HH // WIN, WW // WIN, WIN, WIN, D)
    return split.transpose(0, 2, 1, 3, 4).reshape(1, TOKENS, D)


def exchange(x):
    return lax.all_to_all(x, "frame", split_axis=0, concat_axis=0, tiled=True)


def per_device(latents, cotangent, gain_time, qkv_time, out_time, gain_space, qkv_space, out_space):
    moved = exchange(jnp.concatenate([to_windows(latents), to_windows(cotangent)], axis=1))
    sent = run_main(moved, gain_time, qkv_time, out_time, gain_space, qkv_space, out_space)
    back = exchange(sent).astype(F32)
    grad_latents = from_windows(back[:, :SHARE])
    inverse = 1.0 / jnp.sqrt(jnp.float32(FRAMES * TOKENS))
    sums = jnp.sum(back[:, SHARE:], axis=0) * inverse

    def weights(first):
        qkv = jnp.concatenate([sums[first + 16 * i : first + 16 * (i + 1)] for i in range(3)], axis=1)
        return qkv, sums[first + 48 : first + 64]

    qkv_t, out_t = weights(0)
    qkv_s, out_s = weights(64)
    mine = lax.axis_index("frame") * 16
    gains = lax.dynamic_slice_in_dim(sums[128:130] + sums[130:132], mine, 16, axis=1)
    return (grad_latents, qkv_t, out_t, qkv_s, out_s, gains[0], gains[1])


def solution(mesh):
    whole = P(("dp", "frame"), None, None)
    rows = P(("dp", "frame"), None)
    flat = P(("dp", "frame"))
    return jax.shard_map(
        per_device,
        mesh=mesh,
        in_specs=(whole, whole, P(), P(), P(), P(), P(), P()),
        out_specs=(whole, rows, rows, rows, rows, flat, flat),
        check_vma=False,
    )
```

profile of v0, /device:TPU:1, one launch (start us, length us, event | category | flops | bytes accessed | tf_op | source)
XLA Modules:
  0.0 96.7 jit_solution(2088010897893263678)
XLA Ops:
  0.6 1.1 %copy.15 = bf16[4,8,4,8,256]{4,3,1,2,0:T(8,128)(2,1)S(1)} copy(bf16[4,8,4,8,256]{4,3,2,1,0:T(8,128)(2,1)} %bitcast.24) | data formatting | bytes 1048576 | tf_op jit(solution)/shard_map/reshape | solution.py:269
  1.7 1.1 %copy.16 = bf16[4,8,4,8,256]{4,3,1,2,0:T(8,128)(2,1)S(1)} copy(bf16[4,8,4,8,256]{4,3,2,1,0:T(8,128)(2,1)} %bitcast.25) | data formatting | bytes 1048576 | tf_op jit(solution)/shard_map/reshape | solution.py:269
  2.8 0.0 copy-start
  2.8 0.0 copy-start.1
  2.9 0.0 copy-start.2
  2.9 0.0 copy-start.3
  2.9 0.0 copy-start.4
  2.9 0.0 copy-start.5
  2.9 0.1 pad_maximum_fusion
  3.0 25.3 %all_to_all.10.moved = bf16[16,128,256]{2,1,0:T(8,128)(2,1)S(1)} all-to-all(bf16[16,128,256]{2,1,0:T(8,128)(2,1)S(1)} %pad_maximum_fusion), channel_id=1, replica_groups=mesh['dp'=8,'frame'=16] {'frame'}, dimensions={0} | all-to-all | bytes 2097152 | tf_op jit(solution)/shard_map/all_to_all | solution.py:279
  28.3 0.0 copy-done
  28.3 0.0 copy-done.1
  28.3 0.0 copy-done.2
  28.3 35.8 %shard_map.135 = bf16[16,208,256]{2,1,0:T(8,128)(2,1)} custom-call(bf16[16,128,256]{2,1,0:T(8,128)(2,1)S(1)} %all_to_all.10.moved, f32[1,256]{1,0:T(1,128)S(1)} %bitcast.18, bf16[256,768]{1,0:T(8,128)(2,1)S(1)} %copy-done, bf16[256,256]{1,0:T(8,128)(2,1)S(1)} %copy-done.2, f32[1,256]{1,0:T(1,128)S(1)} %bitcast.19, bf16[256,768]{1,0:T(8,128)(2,1)S(1)} %copy-done.1, ...), custom_call_target="tpu_custom_call" | custom-call | flops 8000000000 | bytes 6000000 | tf_op jit(solution)/shard_map/pallas_call | solution.py:242
  64.1 4.7 %all-to-all-start.1 = ((bf16[16,208,256]{2,1,0:T(8,128)(2,1)}), bf16[16,208,256]{2,1,0:T(8,128)(2,1)S(1)}, u32[]{:S(2)}, u32[]{:S(2)}) async-start(bf16[16,208,256]{2,1,0:T(8,128)(2,1)} %shard_map.135), calls=%async_computation.1 | async-start | bytes 3407872 | tf_op jit(solution)/shard_map/all_to_all | solution.py:279
  68.8 24.3 %all-to-all-done.1 = bf16[16,208,256]{2,1,0:T(8,128)(2,1)S(1)} async-done(((bf16[16,208,256]{2,1,0:T(8,128)(2,1)}), bf16[16,208,256]{2,1,0:T(8,128)(2,1)S(1)}, u32[]{:S(2)}, u32[]{:S(2)}) %all-to-all-start.1) | async-done | bytes 1703968 | tf_op jit(solution)/shard_map/all_to_all | solution.py:279
  93.1 0.3 convert_element_type.3
  93.5 0.2 slice_reduce_fusion
  93.6 0.6 fusion.1
  94.3 0.1 dynamic-slice_add_fusion
  94.3 0.5 slice_bitcast_fusion
  94.9 0.1 slice.56
  95.0 1.1 %copy.17 = f32[4,8,4,8,256]{4,3,2,1,0:T(8,128)} copy(f32[4,8,4,8,256]{4,3,1,2,0:T(8,128)S(1)} %bitcast.20) | data formatting | bytes 2097152 | tf_op jit(solution)/shard_map/transpose | solution.py:275
  96.1 0.6 pad_maximum_fusion.1
  (5 shorter events, 0.0 us)
Async XLA Ops:
  2.8 25.5 %copy-start = (bf16[256,768]{1,0:T(8,128)(2,1)S(1)}, bf16[256,768]{1,0:T(8,128)(2,1)}, u32[]{:S(2)}) copy-start(bf16[256,768]{1,0:T(8,128)(2,1)} %qkv_t.1) | copy-start | bytes 1179652
  2.8 25.5 %copy-start.1 = (bf16[256,768]{1,0:T(8,128)(2,1)S(1)}, bf16[256,768]{1,0:T(8,128)(2,1)}, u32[]{:S(2)}) copy-start(bf16[256,768]{1,0:T(8,128)(2,1)} %qkv_s.1) | copy-start | bytes 1179652
  2.9 25.4 %copy-start.2 = (bf16[256,256]{1,0:T(8,128)(2,1)S(1)}, bf16[256,256]{1,0:T(8,128)(2,1)}, u32[]{:S(2)}) copy-start(bf16[256,256]{1,0:T(8,128)(2,1)} %out_t.1) | copy-start | bytes 393220
  2.9 25.4 %copy-start.3 = (bf16[256,256]{1,0:T(8,128)(2,1)S(1)}, bf16[256,256]{1,0:T(8,128)(2,1)}, u32[]{:S(2)}) copy-start(bf16[256,256]{1,0:T(8,128)(2,1)} %out_s.1) | copy-start | bytes 393220
  2.9 25.4 %copy-start.4 = (f32[256]{0:T(256)S(1)}, f32[256]{0:T(256)}, u32[]{:S(2)}) copy-start(f32[256]{0:T(256)} %param.10) | copy-start | bytes 3076
  2.9 25.4 %copy-start.5 = (f32[256]{0:T(256)S(1)}, f32[256]{0:T(256)}, u32[]{:S(2)}) copy-start(f32[256]{0:T(256)} %param.13) | copy-start | bytes 3076
  64.1 29.0 %all-to-all-start.1 = ((bf16[16,208,256]{2,1,0:T(8,128)(2,1)}), bf16[16,208,256]{2,1,0:T(8,128)(2,1)S(1)}, u32[]{:S(2)}, u32[]{:S(2)}) async-start(bf16[16,208,256]{2,1,0:T(8,128)(2,1)} %shard_map.135), calls=%async_computation.1 | async-start | bytes 3407872 | tf_op jit(solution)/shard_map/all_to_all | solution.py:279
where the time goes:
time: 97 us; the launch traced here: 96.7 us
  Pallas kernels  35.8 us (37%)
  blocking collectives  25.3 us (26%)
  waiting for transfers between devices  24.3 us (25%)
  starting transfers between devices  4.67 us (5%)
  local copies, waits for them, and re-layouts  4.59 us (5%)
  other arithmetic  1.3 us (1%)
    pallas_call x1, Pallas kernels, run_main(): pl.pallas_call(main_kernel, out_shape=jax.ShapeDtypeStruct((FRAMES, 208,...  35.8 us
    all_to_all x1, blocking collectives, exchange(): return lax.all_to_all(x, 'frame', split_axis=0, concat_axis=0, tiled=True)  25.3 us
    all_to_all x1, waiting for transfers between devices, exchange(): return lax.all_to_all(x, 'frame', split_axis=0, concat_axis=0, tiled=True)  24.3 us
    all_to_all x1, starting transfers between devices, exchange(): return lax.all_to_all(x, 'frame', split_axis=0, concat_axis=0, tiled=True)  4.67 us
    reshape x2, local copies, waits for them, and re-layouts, to_windows(): split = frame.reshape(HH // WIN, WIN, WW // WIN, WIN, D)  2.18 us
  transfers between devices with their start and end apart: 1, of which 1 were waited for; matrix products, arithmetic and copies ran while one was open for 0% of the time, Pallas kernels for 0%

commit v1 on v0

v1 whole, which is shorter than its diff:
```python
import jax
import jax.numpy as jnp
from jax import lax
from jax.experimental import pallas as pl
from jax.experimental.pallas import tpu as pltpu
from jax.sharding import PartitionSpec as P

HEADS = 8
HEAD_DIM = 32
D = 256
WIN = 8
HH = 32
WW = 32
FRAMES = 16
TOKENS = 1024
ROWS = 1024
SHARE = 64
GROUP = 128
HALF = 128
PACK = 4
CHUNK = 512
SPACE_STEP = 8
TIME_STEP = 4
EPSILON = 1e-06
SCALE = HEAD_DIM ** (-0.5)
F32 = jnp.float32
BF16 = jnp.bfloat16


def dot_nn(a, b):
    return lax.dot_general(a, b, (((1,), (0,)), ((), ())), preferred_element_type=F32)


def dot_nt(a, b):
    return lax.dot_general(a, b, (((1,), (1,)), ((), ())), preferred_element_type=F32)


def dot_tn(a, b):
    return lax.dot_general(a, b, (((0,), (0,)), ((), ())), preferred_element_type=F32)


def head_masks():
    lane = lax.broadcasted_iota(jnp.int32, (1, HALF), 1) // HEAD_DIM
    return [(lane == h).astype(F32).astype(BF16) for h in range(PACK)]


def spread(x, masks):
    return jnp.concatenate([x * m for m in masks], axis=0)


def spread_full(x, masks):
    low, high = spread(x[:, :HALF], masks), spread(x[:, HALF:], masks)
    zero = jnp.zeros_like(low)
    return jnp.concatenate(
        [jnp.concatenate([low, zero], axis=1), jnp.concatenate([zero, high], axis=1)], axis=0
    )


def flip_space(x):
    parts = []
    for pair in range(2):
        turned = x[:, HALF * pair : HALF * (pair + 1)].T
        parts += [turned[:SHARE], turned[SHARE:]]
    return jnp.concatenate(parts, axis=1)


def flip_time(x):
    turned = x.T
    blocks = [turned[16 * i : 16 * (i + 1)] for i in range(8)]
    lane = lax.broadcasted_iota(jnp.int32, (16, 128), 1) // 16
    for bit in range(3):
        step = 1 << bit
        upper = (lane // step) % 2 == 1
        for i in range(8):
            if not i & step:
                a, b = blocks[i], blocks[i + step]
                blocks[i] = jnp.where(upper, pltpu.roll(b, 16 * step, 1), a)
                blocks[i + step] = jnp.where(upper, b, pltpu.roll(a, 128 - 16 * step, 1))
    return blocks


def softmax_keys(scores, axis):
    scores = scores * SCALE
    ex = jnp.exp(scores - jnp.max(scores, axis=axis, keepdims=True))
    return ex * (1.0 / jnp.sum(ex, axis=axis, keepdims=True))


def score_grad(probs, dprobs, axis):
    weighted = probs * dprobs
    return weighted - probs * jnp.sum(weighted, axis=axis, keepdims=True)


def norm_factor(x):
    return lax.rsqrt(jnp.mean(x * x, -1, keepdims=True) + EPSILON)


def norm_back(dinput, normed, factor, gain):
    scaled = dinput * gain
    return factor * (scaled - normed * jnp.mean(scaled * normed, -1, keepdims=True))


def main_kernel(
    moved, gain_t, qkv_t, out_t, gain_s, qkv_s, out_s, sent,
    stage, xs, in_t, proj_t, probs_t, mixed_t, middle, in_s, proj_s, mixed_s, dmix, dproj, dmid, dmid_b,
):
    masks = head_masks()

    def rows_of(c, size=CHUNK):
        return pl.ds(pl.multiple_of(c * size, size), size)

    def strided(ref, first, count, stride):
        return jnp.concatenate(
            [ref[half, pl.ds(first, count, stride=stride), :] for half in range(2)], axis=1
        )

    def save(ref, rows, x):
        for half in range(2):
            ref[half, rows, :] = x[:, HALF * half : HALF * (half + 1)]

    def widen(f, _):
        save(stage, rows_of(f, SHARE), moved[f, :SHARE, :].astype(F32))
        return _

    lax.fori_loop(0, FRAMES, widen, 0)

    def by_token(ref, c):
        return jnp.concatenate([strided(ref, c * (CHUNK // 16) + i, FRAMES, SHARE) for i in range(CHUNK // 16)], axis=0)

    def by_frame(ref, c):
        return jnp.concatenate([strided(ref, c * (CHUNK // SHARE) + i, SHARE, FRAMES) for i in range(CHUNK // SHARE)], axis=0)

    def project_time(c, _):
        x = by_token(stage, c)
        xs[rows_of(c), :] = x
        inp = (x * norm_factor(x) * gain_t[...]).astype(BF16)
        in_t[rows_of(c), :] = inp
        proj_t[rows_of(c), :] = dot_nn(inp, qkv_t[...]).astype(BF16)
        return _

    lax.fori_loop(0, ROWS // CHUNK, project_time, 0, unroll=True)

    def token(x, s):
        return x[16 * s : 16 * (s + 1)]

    def time_forward(c, _):
        groups = [rows_of(c * TIME_STEP + i, GROUP) for i in range(TIME_STEP)]
        q, k, v = ([proj_t[rows, D * i : D * (i + 1)] for rows in groups] for i in range(3))
        qb = [[spread_full(token(x, s), masks) for s in range(8)] for x in q]
        scores = [jnp.stack([dot_nt(token(x, s), y[s]) for s in range(8)]) for x, y in zip(k, qb)]
        probs = [softmax_keys(x, 1).reshape(GROUP, 128) for x in scores]
        turned = [flip_time(x) for x in probs]
        vb = [[spread_full(token(x, s), masks) for s in range(8)] for x in v]
        mixed = [[dot_nn(x[s].astype(BF16), y[s]) for s in range(8)] for x, y in zip(turned, vb)]
        for n, rows in enumerate(groups):
            probs_t[rows, :] = probs[n].astype(BF16)
            mixed_t[rows, :] = jnp.concatenate(mixed[n], axis=0).astype(BF16)
        return _

    lax.fori_loop(0, ROWS // GROUP // TIME_STEP, time_forward, 0)

    def make_middle(c, _):
        mid = xs[rows_of(c), :] + dot_nn(mixed_t[rows_of(c), :], out_t[...])
        save(stage, rows_of(c), mid.astype(BF16).astype(F32))
        return _

    lax.fori_loop(0, ROWS // CHUNK, make_middle, 0, unroll=True)

    def cots(c):
        return moved[pl.ds(CHUNK // SHARE * c, CHUNK // SHARE), SHARE:, :].reshape(CHUNK, D)

    def project_space(c, _):
        mid = by_frame(stage, c)
        middle[rows_of(c), :] = mid
        inp = (mid * norm_factor(mid) * gain_s[...]).astype(BF16)
        in_s[rows_of(c), :] = inp
        proj_s[rows_of(c), :] = dot_nn(inp, qkv_s[...]).astype(BF16)
        dmix[rows_of(c), :] = dot_nt(cots(c), out_s[...]).astype(BF16)
        return _

    lax.fori_loop(0, ROWS // CHUNK, project_space, 0, unroll=True)

    def space(c, _):
        units = []
        for i in range(SPACE_STEP):
            rows = rows_of(c * SPACE_STEP + i, SHARE)
            units += [(rows, 0), (rows, HALF)]

        def load(ref, offset):
            return [ref[rows, offset + first : offset + first + HALF] for rows, first in units]

        q, k, v, do = load(proj_s, 0), load(proj_s, D), load(proj_s, 2 * D), load(dmix, 0)
        qb = [spread(x, masks) for x in q]
        scores = [dot_nt(x, y) for x, y in zip(k, qb)]
        dob = [spread(x, masks) for x in do]
        dprobs = [dot_nt(x, y) for x, y in zip(v, dob)]
        probs = [softmax_keys(x, 0) for x in scores]
        probs_b = [x.astype(BF16) for x in probs]
        ds = [score_grad(x, y, 0).astype(BF16) for x, y in zip(probs, dprobs)]
        turned = [flip_space(x) for x in probs_b]
        ds_turned = [flip_space(x) for x in ds]
        dv = [dot_nn(x, y) for x, y in zip(probs_b, dob)]
        dk = [dot_nn(x, y) * SCALE for x, y in zip(ds, qb)]
        mixed = [dot_nn(x, spread(y, masks)) for x, y in zip(turned, v)]
        dq = [dot_nn(x, spread(y, masks)) * SCALE for x, y in zip(ds_turned, k)]
        for n, (rows, first) in enumerate(units):
            mixed_s[rows, first : first + HALF] = mixed[n].astype(BF16)
            for i, grad in enumerate((dq, dk, dv)):
                dproj[rows, D * i + first : D * i + first + HALF] = grad[n].astype(BF16)
        return _

    lax.fori_loop(0, FRAMES // SPACE_STEP, space, 0)

    def place(first, sums):
        sums = sums.astype(BF16)
        for i in range(sums.shape[1] // D):
            for d in range(FRAMES):
                sent[d, first + 16 * i : first + 16 * (i + 1), :] = sums[
                    16 * d : 16 * (d + 1), D * i : D * (i + 1)
                ]

    place(128, dot_tn(in_s[...], dproj[...]))
    place(128 + 48, dot_tn(mixed_s[...], moved[:, SHARE:, :].reshape(ROWS, D)))

    def middle_back(c, gain_sum):
        dinput = dot_nt(dproj[rows_of(c), :], qkv_s[...])
        mid = middle[rows_of(c), :]
        factor = norm_factor(mid)
        normed = mid * factor
        save(dmid, rows_of(c), cots(c).astype(F32) + norm_back(dinput, normed, factor, gain_s[...]))
        return gain_sum + jnp.sum(dinput * normed, axis=0, keepdims=True)

    gain_sum_s = lax.fori_loop(0, ROWS // CHUNK, middle_back, jnp.zeros((1, D), F32), unroll=True)

    def mixed_back(c, _):
        dm = by_token(dmid, c).astype(BF16)
        dmid_b[rows_of(c), :] = dm
        dmix[rows_of(c), :] = dot_nt(dm, out_t[...]).astype(BF16)
        return _

    lax.fori_loop(0, ROWS // CHUNK, mixed_back, 0, unroll=True)

    def time_back(c, _):
        groups = [rows_of(c * TIME_STEP + i, GROUP) for i in range(TIME_STEP)]
        q, k, v = ([proj_t[rows, D * i : D * (i + 1)] for rows in groups] for i in range(3))
        do = [dmix[rows, :] for rows in groups]
        probs_b = [probs_t[rows, :] for rows in groups]
        tokens = range(8)
        dob = [[spread_full(token(x, s), masks) for s in tokens] for x in do]
        dprobs = [jnp.stack([dot_nt(token(x, s), y[s]) for s in tokens]) for x, y in zip(v, dob)]
        ds = [
            score_grad(x.astype(F32).reshape(8, 16, 128), y, 1).reshape(GROUP, 128)
            for x, y in zip(probs_b, dprobs)
        ]
        turned = [flip_time(x) for x in ds]
        ds = [x.astype(BF16) for x in ds]
        dv = [[dot_nn(token(x, s), y[s]) for s in tokens] for x, y in zip(probs_b, dob)]
        dk = [
            [dot_nn(token(x, s), spread_full(token(y, s), masks)) * SCALE for s in tokens]
            for x, y in zip(ds, q)
        ]
        dq = [
            [dot_nn(x[s].astype(BF16), spread_full(token(y, s), masks)) * SCALE for s in tokens]
            for x, y in zip(turned, k)
        ]
        for n, rows in enumerate(groups):
            for i, grad in enumerate((dq, dk, dv)):
                dproj[rows, D * i : D * (i + 1)] = jnp.concatenate(grad[n], axis=0).astype(BF16)
        return _

    lax.fori_loop(0, ROWS // GROUP // TIME_STEP, time_back, 0)

    place(64, dot_tn(in_t[...], dproj[...]))
    place(64 + 48, dot_tn(mixed_t[...], dmid_b[...]))

    def input_back(c, gain_sum):
        dinput = dot_nt(dproj[rows_of(c), :], qkv_t[...])
        x = xs[rows_of(c), :]
        factor = norm_factor(x)
        normed = x * factor
        save(stage, rows_of(c), norm_back(dinput, normed, factor, gain_t[...]))
        return gain_sum + jnp.sum(dinput * normed, axis=0, keepdims=True)

    gain_sum_t = lax.fori_loop(0, ROWS // CHUNK, input_back, jnp.zeros((1, D), F32), unroll=True)

    gains = jnp.concatenate([gain_sum_t, gain_sum_s], axis=0)
    high = gains.astype(BF16).astype(F32)
    low = gains - high
    extra = jnp.concatenate([high, low, jnp.zeros((12, D), F32)], axis=0).astype(BF16)

    def restore(f, _):
        for half in range(2):
            dnorm = stage[half, pl.ds(f, SHARE, stride=FRAMES), :]
            total = dmid[half, rows_of(f, SHARE), :] + dnorm
            sent[f, :SHARE, HALF * half : HALF * (half + 1)] = total.astype(BF16)
        sent[f, 192:208, :] = extra
        return _

    lax.fori_loop(0, FRAMES, restore, 0)


def run_main(moved, gain_t, qkv_t, out_t, gain_s, qkv_s, out_s):
    def rows(width, kind):
        return pltpu.VMEM((ROWS, width), kind)

    return pl.pallas_call(
        main_kernel,
        out_shape=jax.ShapeDtypeStruct((FRAMES, 208, D), BF16),
        scratch_shapes=[
            pltpu.VMEM((2, ROWS, HALF), F32),
            rows(D, F32),
            rows(D, BF16),
            rows(3 * D, BF16),
            rows(128, BF16),
            rows(D, BF16),
            rows(D, F32),
            rows(D, BF16),
            rows(3 * D, BF16),
            rows(D, BF16),
            rows(D, BF16),
            rows(3 * D, BF16),
            pltpu.VMEM((2, ROWS, HALF), F32),
            rows(D, BF16),
        ],
        compiler_params=pltpu.CompilerParams(vmem_limit_bytes=40 * 1024 * 1024),
        cost_estimate=pl.CostEstimate(
            flops=8 * 10**9, bytes_accessed=6 * 10**6, transcendentals=2 * 10**6
        ),
    )(moved, gain_t.reshape(1, D), qkv_t, out_t, gain_s.reshape(1, D), qkv_s, out_s)


def to_windows(frame):
    split = frame.reshape(HH // WIN, WIN, WW // WIN, WIN, D)
    return split.transpose(0, 2, 1, 3, 4).reshape(FRAMES, SHARE, D)


def from_windows(windows):
    split = windows.reshape(HH // WIN, WW // WIN, WIN, WIN, D)
    return split.transpose(0, 2, 1, 3, 4).reshape(1, TOKENS, D)


def exchange(x):
    return lax.all_to_all(x, "frame", split_axis=0, concat_axis=0, tiled=True)


def per_device(latents, cotangent, gain_time, qkv_time, out_time, gain_space, qkv_space, out_space):
    moved = exchange(jnp.concatenate([to_windows(latents), to_windows(cotangent)], axis=1))
    sent = run_main(moved, gain_time, qkv_time, out_time, gain_space, qkv_space, out_space)
    back = exchange(sent).astype(F32)
    grad_latents = from_windows(back[:, :SHARE])
    inverse = 1.0 / jnp.sqrt(jnp.float32(FRAMES * TOKENS))
    sums = jnp.sum(back[:, SHARE:], axis=0) * inverse

    def weights(first):
        qkv = jnp.concatenate([sums[first + 16 * i : first + 16 * (i + 1)] for i in range(3)], axis=1)
        return qkv, sums[first + 48 : first + 64]

    qkv_t, out_t = weights(0)
    qkv_s, out_s = weights(64)
    mine = lax.axis_index("frame") * 16
    gains = lax.dynamic_slice_in_dim(sums[128:130] + sums[130:132], mine, 16, axis=1)
    return (grad_latents, qkv_t, out_t, qkv_s, out_s, gains[0], gains[1])


def solution(mesh):
    whole = P(("dp", "frame"), None, None)
    rows = P(("dp", "frame"), None)
    flat = P(("dp", "frame"))
    return jax.shard_map(
        per_device,
        mesh=mesh,
        in_specs=(whole, whole, P(), P(), P(), P(), P(), P()),
        out_specs=(whole, rows, rows, rows, rows, flat, flat),
        check_vma=False,
    )
```

time: 97 us -> 78.6 us (0.81)
  Pallas kernels: 35.8 us -> 17.3 us
    pallas_call x1, Pallas kernels: 35.8 us -> 17.3 us  [run_main(): pl.pallas_call(main_kernel, out_shape=jax.ShapeDtypeStruct((FRAMES, 208,...]
where the time goes in v1:
time: 78.6 us; the launch traced here: 78.2 us
  blocking collectives  25.3 us (32%)
  waiting for transfers between devices  24.3 us (31%)
  Pallas kernels  17.3 us (22%)
  starting transfers between devices  4.67 us (6%)
  local copies, waits for them, and re-layouts  4.59 us (6%)
  other arithmetic  1.3 us (2%)
    all_to_all x1, blocking collectives, exchange(): return lax.all_to_all(x, 'frame', split_axis=0, concat_axis=0, tiled=True)  25.3 us
    all_to_all x1, waiting for transfers between devices, exchange(): return lax.all_to_all(x, 'frame', split_axis=0, concat_axis=0, tiled=True)  24.3 us
    pallas_call x1, Pallas kernels, run_main(): pl.pallas_call(main_kernel, out_shape=jax.ShapeDtypeStruct((FRAMES, 208,...  17.3 us
    all_to_all x1, starting transfers between devices, exchange(): return lax.all_to_all(x, 'frame', split_axis=0, concat_axis=0, tiled=True)  4.67 us
    reshape x2, local copies, waits for them, and re-layouts, to_windows(): split = frame.reshape(HH // WIN, WIN, WW // WIN, WIN, D)  2.18 us
  transfers between devices with their start and end apart: 1, of which 1 were waited for; matrix products, arithmetic and copies ran while one was open for 0% of the time, Pallas kernels for 0%

profile of v1, /device:TPU:1, one launch (start us, length us, event | category | flops | bytes accessed | tf_op | source)
XLA Modules:
  0.0 78.2 jit_solution(10896484288752822444)
XLA Ops:
  0.6 1.1 %copy.15 = bf16[4,8,4,8,256]{4,3,1,2,0:T(8,128)(2,1)S(1)} copy(bf16[4,8,4,8,256]{4,3,2,1,0:T(8,128)(2,1)} %bitcast.24) | data formatting | bytes 1048576 | tf_op jit(solution)/shard_map/reshape | solution.py:332
  1.7 1.1 %copy.16 = bf16[4,8,4,8,256]{4,3,1,2,0:T(8,128)(2,1)S(1)} copy(bf16[4,8,4,8,256]{4,3,2,1,0:T(8,128)(2,1)} %bitcast.25) | data formatting | bytes 1048576 | tf_op jit(solution)/shard_map/reshape | solution.py:332
  2.8 0.0 copy-start
  2.8 0.0 copy-start.1
  2.9 0.0 copy-start.2
  2.9 0.0 copy-start.3
  2.9 0.0 copy-start.4
  2.9 0.0 copy-start.5
  2.9 0.1 pad_maximum_fusion
  3.0 25.3 %all_to_all.10.moved = bf16[16,128,256]{2,1,0:T(8,128)(2,1)S(1)} all-to-all(bf16[16,128,256]{2,1,0:T(8,128)(2,1)S(1)} %pad_maximum_fusion), channel_id=1, replica_groups=mesh['dp'=8,'frame'=16] {'frame'}, dimensions={0} | all-to-all | bytes 2097152 | tf_op jit(solution)/shard_map/all_to_all | solution.py:342
  28.3 0.0 copy-done
  28.3 0.0 copy-done.1
  28.3 0.0 copy-done.2
  28.3 17.3 %shard_map.135 = bf16[16,208,256]{2,1,0:T(8,128)(2,1)} custom-call(bf16[16,128,256]{2,1,0:T(8,128)(2,1)S(1)} %all_to_all.10.moved, f32[1,256]{1,0:T(1,128)S(1)} %bitcast.18, bf16[256,768]{1,0:T(8,128)(2,1)S(1)} %copy-done, bf16[256,256]{1,0:T(8,128)(2,1)S(1)} %copy-done.2, f32[1,256]{1,0:T(1,128)S(1)} %bitcast.19, bf16[256,768]{1,0:T(8,128)(2,1)S(1)} %copy-done.1, ...), custom_call_target="tpu_custom_call" | custom-call | flops 8000000000 | bytes 6000000 | tf_op jit(solution)/shard_map/pallas_call | solution.py:305
  45.6 4.7 %all-to-all-start.1 = ((bf16[16,208,256]{2,1,0:T(8,128)(2,1)}), bf16[16,208,256]{2,1,0:T(8,128)(2,1)S(1)}, u32[]{:S(2)}, u32[]{:S(2)}) async-start(bf16[16,208,256]{2,1,0:T(8,128)(2,1)} %shard_map.135), calls=%async_computation.1 | async-start | bytes 3407872 | tf_op jit(solution)/shard_map/all_to_all | solution.py:342
  50.3 24.3 %all-to-all-done.1 = bf16[16,208,256]{2,1,0:T(8,128)(2,1)S(1)} async-done(((bf16[16,208,256]{2,1,0:T(8,128)(2,1)}), bf16[16,208,256]{2,1,0:T(8,128)(2,1)S(1)}, u32[]{:S(2)}, u32[]{:S(2)}) %all-to-all-start.1) | async-done | bytes 1703968 | tf_op jit(solution)/shard_map/all_to_all | solution.py:342
  74.6 0.3 convert_element_type.3
  75.0 0.2 slice_reduce_fusion
  75.1 0.6 fusion.1
  75.8 0.1 dynamic-slice_add_fusion
  75.8 0.5 slice_bitcast_fusion
  76.4 0.1 slice.56
  76.5 1.1 %copy.17 = f32[4,8,4,8,256]{4,3,2,1,0:T(8,128)} copy(f32[4,8,4,8,256]{4,3,1,2,0:T(8,128)S(1)} %bitcast.20) | data formatting | bytes 2097152 | tf_op jit(solution)/shard_map/transpose | solution.py:338
  77.6 0.6 pad_maximum_fusion.1
  (5 shorter events, 0.0 us)
Async XLA Ops:
  2.8 25.5 %copy-start = (bf16[256,768]{1,0:T(8,128)(2,1)S(1)}, bf16[256,768]{1,0:T(8,128)(2,1)}, u32[]{:S(2)}) copy-start(bf16[256,768]{1,0:T(8,128)(2,1)} %qkv_t.1) | copy-start | bytes 1179652
  2.8 25.5 %copy-start.1 = (bf16[256,768]{1,0:T(8,128)(2,1)S(1)}, bf16[256,768]{1,0:T(8,128)(2,1)}, u32[]{:S(2)}) copy-start(bf16[256,768]{1,0:T(8,128)(2,1)} %qkv_s.1) | copy-start | bytes 1179652
  2.9 25.4 %copy-start.2 = (bf16[256,256]{1,0:T(8,128)(2,1)S(1)}, bf16[256,256]{1,0:T(8,128)(2,1)}, u32[]{:S(2)}) copy-start(bf16[256,256]{1,0:T(8,128)(2,1)} %out_t.1) | copy-start | bytes 393220
  2.9 25.4 %copy-start.3 = (bf16[256,256]{1,0:T(8,128)(2,1)S(1)}, bf16[256,256]{1,0:T(8,128)(2,1)}, u32[]{:S(2)}) copy-start(bf16[256,256]{1,0:T(8,128)(2,1)} %out_s.1) | copy-start | bytes 393220
  2.9 25.4 %copy-start.4 = (f32[256]{0:T(256)S(1)}, f32[256]{0:T(256)}, u32[]{:S(2)}) copy-start(f32[256]{0:T(256)} %param.10) | copy-start | bytes 3076
  2.9 25.4 %copy-start.5 = (f32[256]{0:T(256)S(1)}, f32[256]{0:T(256)}, u32[]{:S(2)}) copy-start(f32[256]{0:T(256)} %param.13) | copy-start | bytes 3076
  45.6 29.0 %all-to-all-start.1 = ((bf16[16,208,256]{2,1,0:T(8,128)(2,1)}), bf16[16,208,256]{2,1,0:T(8,128)(2,1)S(1)}, u32[]{:S(2)}, u32[]{:S(2)}) async-start(bf16[16,208,256]{2,1,0:T(8,128)(2,1)} %shard_map.135), calls=%async_computation.1 | async-start | bytes 3407872 | tf_op jit(solution)/shard_map/all_to_all | solution.py:342

commit v2 on v1

--- a/solution.py
+++ b/solution.py
@@ -19,8 +19,8 @@
 HALF = 128
 PACK = 4
 CHUNK = 512
-SPACE_STEP = 8
-TIME_STEP = 4
+SPACE_STEP = 16
+TIME_STEP = 8
 EPSILON = 1e-06
 SCALE = HEAD_DIM ** (-0.5)
 F32 = jnp.float32
@@ -285,14 +285,16 @@
     gains = jnp.concatenate([gain_sum_t, gain_sum_s], axis=0)
     high = gains.astype(BF16).astype(F32)
     low = gains - high
-    extra = jnp.concatenate([high, low, jnp.zeros((12, D), F32)], axis=0).astype(BF16)
+    extra = jnp.concatenate([high, low, jnp.zeros((12, D), F32)], axis=0)
+    for d in range(FRAMES):
+        turned = extra if d == 0 else pltpu.roll(extra, D - 16 * d, 1)
+        sent[d, 192:208, :] = turned.astype(BF16)
 
     def restore(f, _):
         for half in range(2):
             dnorm = stage[half, pl.ds(f, SHARE, stride=FRAMES), :]
             total = dmid[half, rows_of(f, SHARE), :] + dnorm
             sent[f, :SHARE, HALF * half : HALF * (half + 1)] = total.astype(BF16)
-        sent[f, 192:208, :] = extra
         return _
 
     lax.fori_loop(0, FRAMES, restore, 0)
@@ -328,14 +330,56 @@
     )(moved, gain_t.reshape(1, D), qkv_t, out_t, gain_s.reshape(1, D), qkv_s, out_s)
 
 
-def to_windows(frame):
-    split = frame.reshape(HH // WIN, WIN, WW // WIN, WIN, D)
-    return split.transpose(0, 2, 1, 3, 4).reshape(FRAMES, SHARE, D)
-
-
-def from_windows(windows):
-    split = windows.reshape(HH // WIN, WW // WIN, WIN, WIN, D)
-    return split.transpose(0, 2, 1, 3, 4).reshape(1, TOKENS, D)
+def pack_kernel(latents, cotangent, packed):
+    for wy in range(4):
+        for pair in range(4):
+            first = 64 * (4 * wy + pair)
+            for src, base in ((latents, 0), (cotangent, SHARE)):
+                rows = src[0, first : first + 64, :].astype(F32).reshape(2, 4, WIN, D)
+                for wx in range(4):
+                    both = jnp.concatenate([rows[0, wx], rows[1, wx]], axis=0).astype(BF16)
+                    packed[4 * wy + wx, base + 16 * pair : base + 16 * (pair + 1), :] = both
+
+
+def pack(latents, cotangent):
+    return pl.pallas_call(
+        pack_kernel,
+        out_shape=jax.ShapeDtypeStruct((FRAMES, 2 * SHARE, D), BF16),
+    )(latents, cotangent)
+
+
+def unpack_kernel(back, grads, qkv_t, out_t, qkv_s, out_s, gains):
+    for wy in range(4):
+        for pair in range(4):
+            rows = back[4 * wy : 4 * wy + 4, 16 * pair : 16 * (pair + 1), :].astype(F32)
+            first = 64 * (4 * wy + pair)
+            for wx in range(4):
+                for i in range(2):
+                    start = first + 32 * i + WIN * wx
+                    grads[0, start : start + WIN, :] = rows[wx, WIN * i : WIN * (i + 1)]
+    inverse = (FRAMES * TOKENS) ** (-0.5)
+
+    def total(first):
+        return jnp.sum(back[:, first : first + 16, :].astype(F32), axis=0) * inverse
+
+    for first, qkv, out in ((SHARE, qkv_t, out_t), (2 * SHARE, qkv_s, out_s)):
+        for i in range(3):
+            qkv[:, D * i : D * (i + 1)] = total(first + 16 * i)
+        out[...] = total(first + 48)
+    sums = total(192)
+    gains[...] = sums[0:2, :128] + sums[2:4, :128]
+
+
+def unpack(back):
+    def out(*shape):
+        return jax.ShapeDtypeStruct(shape, F32)
+
+    return pl.pallas_call(
+        unpack_kernel,
+        out_shape=(
+            out(1, TOKENS, D), out(16, 3 * D), out(16, D), out(16, 3 * D), out(16, D), out(2, 128)
+        ),
+    )(back)
 
 
 def exchange(x):
@@ -343,22 +387,10 @@
 
 
 def per_device(latents, cotangent, gain_time, qkv_time, out_time, gain_space, qkv_space, out_space):
-    moved = exchange(jnp.concatenate([to_windows(latents), to_windows(cotangent)], axis=1))
+    moved = exchange(pack(latents, cotangent))
     sent = run_main(moved, gain_time, qkv_time, out_time, gain_space, qkv_space, out_space)
-    back = exchange(sent).astype(F32)
-    grad_latents = from_windows(back[:, :SHARE])
-    inverse = 1.0 / jnp.sqrt(jnp.float32(FRAMES * TOKENS))
-    sums = jnp.sum(back[:, SHARE:], axis=0) * inverse
-
-    def weights(first):
-        qkv = jnp.concatenate([sums[first + 16 * i : first + 16 * (i + 1)] for i in range(3)], axis=1)
-        return qkv, sums[first + 48 : first + 64]
-
-    qkv_t, out_t = weights(0)
-    qkv_s, out_s = weights(64)
-    mine = lax.axis_index("frame") * 16
-    gains = lax.dynamic_slice_in_dim(sums[128:130] + sums[130:132], mine, 16, axis=1)
-    return (grad_latents, qkv_t, out_t, qkv_s, out_s, gains[0], gains[1])
+    *grads, gains = unpack(exchange(sent))
+    return (*grads, gains[0, :16], gains[1, :16])
 
 
 def solution(mesh):

time: 78.6 us -> 76.4 us (0.972)
  blocking collectives: 25.3 us -> 54.2 us
  waiting for transfers between devices: 24.3 us -> 0 us
  starting transfers between devices: 4.67 us -> 0 us
  local copies, waits for them, and re-layouts: 4.59 us -> 1.3 us
  Pallas kernels: 17.3 us -> 19.9 us
  other arithmetic: 1.3 us -> 0 us
    all_to_all x1 -> x2, blocking collectives: 25.3 us -> 54.2 us  [exchange(): return lax.all_to_all(x, 'frame', split_axis=0, concat_axis=0, tiled=True)]
    all_to_all x1 -> x0, waiting for transfers between devices: 24.3 us -> none  [exchange(): return lax.all_to_all(x, 'frame', split_axis=0, concat_axis=0, tiled=True)]
    pallas_call x0 -> x2, Pallas kernels: none -> 4.92 us  [the longest x1 2.6 us: unpack(): pl.pallas_call(unpack_kernel, out_shape=(out(1, TOKENS, D), out(16, 3 * D...]
    all_to_all x1 -> x0, starting transfers between devices: 4.67 us -> none  [exchange(): return lax.all_to_all(x, 'frame', split_axis=0, concat_axis=0, tiled=True)]
    pallas_call x1, Pallas kernels: 17.3 us -> 15 us  [run_main(): pl.pallas_call(main_kernel, out_shape=jax.ShapeDtypeStruct((FRAMES, 208,...]
    reshape x2 -> x0, local copies, waits for them, and re-layouts: 2.18 us -> none  [to_windows(): split = frame.reshape(HH // WIN, WIN, WW // WIN, WIN, D)]
    transpose x1 -> x0, local copies, waits for them, and re-layouts: 1.12 us -> none  [from_windows(): return split.transpose(0, 2, 1, 3, 4).reshape(1, TOKENS, D)]
  transfers between devices with their start and end apart: 1 -> 0, of which waited for: 1 -> 0; matrix products, arithmetic and copies ran while one was open for 0% -> 0% of each run, Pallas kernels for 0% -> 0%
where the time goes in v2:
time: 76.4 us; the launch traced here: 76.1 us
  blocking collectives  54.2 us (71%)
  Pallas kernels  19.9 us (26%)
  local copies, waits for them, and re-layouts  1.3 us (2%)
    all_to_all x2, blocking collectives, exchange(): return lax.all_to_all(x, 'frame', split_axis=0, concat_axis=0, tiled=True)  54.2 us
    pallas_call x1, Pallas kernels, run_main(): pl.pallas_call(main_kernel, out_shape=jax.ShapeDtypeStruct((FRAMES, 208,...  15 us
    pallas_call x1, Pallas kernels, unpack(): pl.pallas_call(unpack_kernel, out_shape=(out(1, TOKENS, D), out(16, 3 * D...  2.6 us
    pallas_call x1, Pallas kernels, pack(): pl.pallas_call(pack_kernel, out_shape=jax.ShapeDtypeStruct((FRAMES, 2 * S...  2.32 us

profile of v2, /device:TPU:1, one launch (start us, length us, event | category | flops | bytes accessed | tf_op | source)
XLA Modules:
  0.0 76.1 jit_solution(3906197361362080988)
XLA Ops:
  0.6 0.0 copy-start.3
  0.6 0.0 copy-start.1
  0.7 0.0 copy-start.5
  0.7 0.0 copy-start.2
  0.7 0.0 copy-start
  0.7 0.0 copy-start.4
  0.7 2.3 %shard_map.135 = bf16[16,128,256]{2,1,0:T(8,128)(2,1)} custom-call(bf16[1,1024,256]{2,1,0:T(8,128)(2,1)} %latents.1, bf16[1,1024,256]{2,1,0:T(8,128)(2,1)} %cotangent.1), custom_call_target="tpu_custom_call" | custom-call | tf_op jit(solution)/shard_map/pallas_call | solution.py:345
  3.0 25.4 %all_to_all.10.moved = bf16[16,128,256]{2,1,0:T(8,128)(2,1)S(1)} all-to-all(bf16[16,128,256]{2,1,0:T(8,128)(2,1)} %shard_map.135), channel_id=1, replica_groups=mesh['dp'=8,'frame'=16] {'frame'}, dimensions={0} | all-to-all | bytes 2097152 | tf_op jit(solution)/shard_map/all_to_all | solution.py:386
  28.4 0.0 copy-done.3
  28.4 0.0 copy-done.1
  28.4 0.0 copy-done.5
  28.4 0.0 copy-done.2
  28.4 0.0 copy-done
  28.4 0.0 copy-done.4
  28.4 15.0 %shard_map.136 = bf16[16,208,256]{2,1,0:T(8,128)(2,1)S(1)} custom-call(bf16[16,128,256]{2,1,0:T(8,128)(2,1)S(1)} %all_to_all.10.moved, f32[1,256]{1,0:T(1,128)S(1)} %bitcast.6, bf16[256,768]{1,0:T(8,128)(2,1)S(1)} %copy-done, bf16[256,256]{1,0:T(8,128)(2,1)S(1)} %copy-done.2, f32[1,256]{1,0:T(1,128)S(1)} %bitcast.7, bf16[256,768]{1,0:T(8,128)(2,1)S(1)} %copy-done.1, ...), custom_call_target="tpu_custom_call" | custom-call | flops 8000000000 | bytes 6000000 | tf_op jit(solution)/shard_map/pallas_call | solution.py:307
  43.4 28.9 %all_to_all.11.back = bf16[16,208,256]{2,1,0:T(8,128)(2,1)} all-to-all(bf16[16,208,256]{2,1,0:T(8,128)(2,1)S(1)} %shard_map.136), channel_id=1, replica_groups=mesh['dp'=8,'frame'=16] {'frame'}, dimensions={0} | all-to-all | bytes 3407872 | tf_op jit(solution)/shard_map/all_to_all | solution.py:386
  72.3 2.6 %shard_map.137 = (f32[1,1024,256]{2,1,0:T(8,128)}, f32[16,768]{1,0:T(8,128)}, f32[16,256]{1,0:T(8,128)}, f32[16,768]{1,0:T(8,128)}, f32[16,256]{1,0:T(8,128)}, /*index=5*/f32[2,128]{1,0:T(2,128)}) custom-call(bf16[16,208,256]{2,1,0:T(8,128)(2,1)} %all_to_all.11.back), custom_call_target="tpu_custom_call" | custom-call | tf_op jit(solution)/shard_map/pallas_call | solution.py:377
  74.9 1.3 %slice_bitcast_fusion = (f32[16]{0:T(128)}, f32[16]{0:T(128)}) fusion(f32[2,128]{1,0:T(2,128)} %get-tuple-element.18), kind=kLoop, calls=%fused_computation | loop fusion | bytes 256 | tf_op jit(solution)/shard_map/squeeze | solution.py:393
Async XLA Ops:
  0.6 27.7 %copy-start.3 = (bf16[256,256]{1,0:T(8,128)(2,1)S(1)}, bf16[256,256]{1,0:T(8,128)(2,1)}, u32[]{:S(2)}) copy-start(bf16[256,256]{1,0:T(8,128)(2,1)} %out_s.1) | copy-start | bytes 393220
  0.6 27.7 %copy-start.1 = (bf16[256,768]{1,0:T(8,128)(2,1)S(1)}, bf16[256,768]{1,0:T(8,128)(2,1)}, u32[]{:S(2)}) copy-start(bf16[256,768]{1,0:T(8,128)(2,1)} %qkv_s.1) | copy-start | bytes 1179652
  0.7 27.7 %copy-start.5 = (f32[256]{0:T(256)S(1)}, f32[256]{0:T(256)}, u32[]{:S(2)}) copy-start(f32[256]{0:T(256)} %param.13) | copy-start | bytes 3076
  0.7 27.7 %copy-start.2 = (bf16[256,256]{1,0:T(8,128)(2,1)S(1)}, bf16[256,256]{1,0:T(8,128)(2,1)}, u32[]{:S(2)}) copy-start(bf16[256,256]{1,0:T(8,128)(2,1)} %out_t.1) | copy-start | bytes 393220
  0.7 27.7 %copy-start = (bf16[256,768]{1,0:T(8,128)(2,1)S(1)}, bf16[256,768]{1,0:T(8,128)(2,1)}, u32[]{:S(2)}) copy-start(bf16[256,768]{1,0:T(8,128)(2,1)} %qkv_t.1) | copy-start | bytes 1179652
  0.7 27.7 %copy-start.4 = (f32[256]{0:T(256)S(1)}, f32[256]{0:T(256)}, u32[]{:S(2)}) copy-start(f32[256]{0:T(256)} %param.10) | copy-start | bytes 3076

commit v3 on v2

--- a/solution.py
+++ b/solution.py
@@ -99,23 +99,25 @@
     return factor * (scaled - normed * jnp.mean(scaled * normed, -1, keepdims=True))
 
 
+def rows_of(c, size=CHUNK):
+    return pl.ds(pl.multiple_of(c * size, size), size)
+
+
+def save(ref, rows, x):
+    for half in range(2):
+        ref[half, rows, :] = x[:, HALF * half : HALF * (half + 1)]
+
+
 def main_kernel(
-    moved, gain_t, qkv_t, out_t, gain_s, qkv_s, out_s, sent,
-    stage, xs, in_t, proj_t, probs_t, mixed_t, middle, in_s, proj_s, mixed_s, dmix, dproj, dmid, dmid_b,
+    moved, gain_t, qkv_t, out_t, gain_s, qkv_s, out_s, xs, dproj, dmid, gain_sum_s, kept, given,
+    stage, in_t, proj_t, probs_t, mixed_t, middle, in_s, proj_s, mixed_s, dmix, dmid_b, parts,
 ):
     masks = head_masks()
-
-    def rows_of(c, size=CHUNK):
-        return pl.ds(pl.multiple_of(c * size, size), size)
 
     def strided(ref, first, count, stride):
         return jnp.concatenate(
             [ref[half, pl.ds(first, count, stride=stride), :] for half in range(2)], axis=1
         )
-
-    def save(ref, rows, x):
-        for half in range(2):
-            ref[half, rows, :] = x[:, HALF * half : HALF * (half + 1)]
 
     def widen(f, _):
         save(stage, rows_of(f, SHARE), moved[f, :SHARE, :].astype(F32))
@@ -210,16 +212,16 @@
 
     lax.fori_loop(0, FRAMES // SPACE_STEP, space, 0)
 
-    def place(first, sums):
+    def place(kind, first, sums):
         sums = sums.astype(BF16)
         for i in range(sums.shape[1] // D):
             for d in range(FRAMES):
-                sent[d, first + 16 * i : first + 16 * (i + 1), :] = sums[
+                parts[kind, d, first + 16 * i : first + 16 * (i + 1), :] = sums[
                     16 * d : 16 * (d + 1), D * i : D * (i + 1)
                 ]
 
-    place(128, dot_tn(in_s[...], dproj[...]))
-    place(128 + 48, dot_tn(mixed_s[...], moved[:, SHARE:, :].reshape(ROWS, D)))
+    place(1, 0, dot_tn(in_s[...], dproj[...]))
+    place(1, 48, dot_tn(mixed_s[...], moved[:, SHARE:, :].reshape(ROWS, D)))
 
     def middle_back(c, gain_sum):
         dinput = dot_nt(dproj[rows_of(c), :], qkv_s[...])
@@ -229,7 +231,7 @@
         save(dmid, rows_of(c), cots(c).astype(F32) + norm_back(dinput, normed, factor, gain_s[...]))
         return gain_sum + jnp.sum(dinput * normed, axis=0, keepdims=True)
 
-    gain_sum_s = lax.fori_loop(0, ROWS // CHUNK, middle_back, jnp.zeros((1, D), F32), unroll=True)
+    gain_sum_s[...] = lax.fori_loop(0, ROWS // CHUNK, middle_back, jnp.zeros((1, D), F32), unroll=True)
 
     def mixed_back(c, _):
         dm = by_token(dmid, c).astype(BF16)
@@ -269,9 +271,15 @@
 
     lax.fori_loop(0, ROWS // GROUP // TIME_STEP, time_back, 0)
 
-    place(64, dot_tn(in_t[...], dproj[...]))
-    place(64 + 48, dot_tn(mixed_t[...], dmid_b[...]))
-
+    place(0, 0, dot_tn(in_t[...], dproj[...]))
+    place(0, 48, dot_tn(mixed_t[...], dmid_b[...]))
+
+    core = lax.axis_index("frame") % 2
+    kept[...] = parts[core]
+    given[...] = parts[1 - core]
+
+
+def input_kernel(xs, dproj, dmid, gain_sum_s, gain_t, qkv_t, sent, stage):
     def input_back(c, gain_sum):
         dinput = dot_nt(dproj[rows_of(c), :], qkv_t[...])
         x = xs[rows_of(c), :]
@@ -282,22 +290,30 @@
 
     gain_sum_t = lax.fori_loop(0, ROWS // CHUNK, input_back, jnp.zeros((1, D), F32), unroll=True)
 
-    gains = jnp.concatenate([gain_sum_t, gain_sum_s], axis=0)
+    gains = jnp.concatenate([gain_sum_t, gain_sum_s[...]], axis=0)
     high = gains.astype(BF16).astype(F32)
     low = gains - high
     extra = jnp.concatenate([high, low, jnp.zeros((12, D), F32)], axis=0)
-    for d in range(FRAMES):
-        turned = extra if d == 0 else pltpu.roll(extra, D - 16 * d, 1)
-        sent[d, 192:208, :] = turned.astype(BF16)
-
-    def restore(f, _):
+    for f in range(FRAMES):
+        turned = extra if f == 0 else pltpu.roll(extra, D - 16 * f, 1)
+        sent[f, SHARE:, :] = turned.astype(BF16)
         for half in range(2):
             dnorm = stage[half, pl.ds(f, SHARE, stride=FRAMES), :]
-            total = dmid[half, rows_of(f, SHARE), :] + dnorm
+            total = dmid[half, SHARE * f : SHARE * (f + 1), :] + dnorm
             sent[f, :SHARE, HALF * half : HALF * (half + 1)] = total.astype(BF16)
-        return _
-
-    lax.fori_loop(0, FRAMES, restore, 0)
+
+
+def join_kernel(grads, kept, taken, sent):
+    sent[:, : SHARE + 16, :] = grads[...]
+    sent[:, SHARE + 16 :, :] = (kept[...].astype(F32) + taken[...].astype(F32)).astype(BF16)
+
+
+def shaped(kind, *shape):
+    return jax.ShapeDtypeStruct(shape, kind)
+
+
+def params(mebibytes):
+    return pltpu.CompilerParams(vmem_limit_bytes=mebibytes * 1024 * 1024)
 
 
 def run_main(moved, gain_t, qkv_t, out_t, gain_s, qkv_s, out_s):
@@ -306,10 +322,16 @@
 
     return pl.pallas_call(
         main_kernel,
-        out_shape=jax.ShapeDtypeStruct((FRAMES, 208, D), BF16),
+        out_shape=(
+            shaped(F32, ROWS, D),
+            shaped(BF16, ROWS, 3 * D),
+            shaped(F32, 2, ROWS, HALF),
+            shaped(F32, 1, D),
+            shaped(BF16, FRAMES, SHARE, D),
+            shaped(BF16, FRAMES, SHARE, D),
+        ),
         scratch_shapes=[
             pltpu.VMEM((2, ROWS, HALF), F32),
-            rows(D, F32),
             rows(D, BF16),
             rows(3 * D, BF16),
             rows(128, BF16),
@@ -319,66 +341,116 @@
             rows(3 * D, BF16),
             rows(D, BF16),
             rows(D, BF16),
-            rows(3 * D, BF16),
-            pltpu.VMEM((2, ROWS, HALF), F32),
-            rows(D, BF16),
+            rows(D, BF16),
+            pltpu.VMEM((2, FRAMES, SHARE, D), BF16),
         ],
-        compiler_params=pltpu.CompilerParams(vmem_limit_bytes=40 * 1024 * 1024),
+        compiler_params=params(40),
         cost_estimate=pl.CostEstimate(
             flops=8 * 10**9, bytes_accessed=6 * 10**6, transcendentals=2 * 10**6
         ),
-    )(moved, gain_t.reshape(1, D), qkv_t, out_t, gain_s.reshape(1, D), qkv_s, out_s)
-
-
-def pack_kernel(latents, cotangent, packed):
+    )(moved, gain_t, qkv_t, out_t, gain_s, qkv_s, out_s)
+
+
+def run_input(xs, dproj, dmid, gain_sum_s, gain_t, qkv_t):
+    return pl.pallas_call(
+        input_kernel,
+        out_shape=shaped(BF16, FRAMES, SHARE + 16, D),
+        scratch_shapes=[pltpu.VMEM((2, ROWS, HALF), F32)],
+        compiler_params=params(16),
+        cost_estimate=pl.CostEstimate(flops=2 * 10**9, bytes_accessed=6 * 10**6, transcendentals=0),
+    )(xs, dproj, dmid, gain_sum_s, gain_t, qkv_t)
+
+
+def join(grads, kept, taken):
+    return pl.pallas_call(
+        join_kernel,
+        out_shape=shaped(BF16, FRAMES, 2 * SHARE + 16, D),
+        compiler_params=params(8),
+    )(grads, kept, taken)
+
+
+def pack_kernel(latents, cotangent, packed, held, sems):
+    copies = [
+        pltpu.make_async_copy(
+            src.at[0, pl.ds(256 * wy, 256)], held.at[n, wy], sems.at[n, wy]
+        )
+        for wy in range(4)
+        for n, src in enumerate((latents, cotangent))
+    ]
+    for copy in copies:
+        copy.start()
     for wy in range(4):
-        for pair in range(4):
-            first = 64 * (4 * wy + pair)
-            for src, base in ((latents, 0), (cotangent, SHARE)):
-                rows = src[0, first : first + 64, :].astype(F32).reshape(2, 4, WIN, D)
+        for n in range(2):
+            copies[2 * wy + n].wait()
+            for pair in range(4):
+                rows = held[n, wy, 64 * pair : 64 * (pair + 1), :].astype(F32).reshape(2, 4, WIN, D)
                 for wx in range(4):
                     both = jnp.concatenate([rows[0, wx], rows[1, wx]], axis=0).astype(BF16)
-                    packed[4 * wy + wx, base + 16 * pair : base + 16 * (pair + 1), :] = both
+                    first = SHARE * n + 16 * pair
+                    packed[4 * wy + wx, first : first + 16, :] = both
 
 
 def pack(latents, cotangent):
     return pl.pallas_call(
         pack_kernel,
-        out_shape=jax.ShapeDtypeStruct((FRAMES, 2 * SHARE, D), BF16),
+        in_specs=[pl.BlockSpec(memory_space=pltpu.HBM)] * 2,
+        out_shape=shaped(BF16, FRAMES, 2 * SHARE, D),
+        scratch_shapes=[
+            pltpu.VMEM((2, 4, 256, D), BF16),
+            pltpu.SemaphoreType.DMA((2, 4)),
+        ],
+        compiler_params=params(8),
     )(latents, cotangent)
 
 
-def unpack_kernel(back, grads, qkv_t, out_t, qkv_s, out_s, gains):
+def unpack_kernel(back, grads, qkv_t, out_t, qkv_s, out_s, gain_t, gain_s, held, sems):
+    copies = []
     for wy in range(4):
         for pair in range(4):
             rows = back[4 * wy : 4 * wy + 4, 16 * pair : 16 * (pair + 1), :].astype(F32)
-            first = 64 * (4 * wy + pair)
             for wx in range(4):
                 for i in range(2):
-                    start = first + 32 * i + WIN * wx
-                    grads[0, start : start + WIN, :] = rows[wx, WIN * i : WIN * (i + 1)]
+                    start = 64 * pair + 32 * i + WIN * wx
+                    held[wy, start : start + WIN, :] = rows[wx, WIN * i : WIN * (i + 1)]
+        copies.append(
+            pltpu.make_async_copy(held.at[wy], grads.at[0, pl.ds(256 * wy, 256)], sems.at[wy])
+        )
+        copies[wy].start()
     inverse = (FRAMES * TOKENS) ** (-0.5)
 
-    def total(first):
-        return jnp.sum(back[:, first : first + 16, :].astype(F32), axis=0) * inverse
-
-    for first, qkv, out in ((SHARE, qkv_t, out_t), (2 * SHARE, qkv_s, out_s)):
+    def total(first, sources):
+        return sum(back[f, first : first + 16, :].astype(F32) for f in sources) * inverse
+
+    for core, qkv, out in ((0, qkv_t, out_t), (1, qkv_s, out_s)):
+        sources = range(core, FRAMES, 2)
         for i in range(3):
-            qkv[:, D * i : D * (i + 1)] = total(first + 16 * i)
-        out[...] = total(first + 48)
-    sums = total(192)
-    gains[...] = sums[0:2, :128] + sums[2:4, :128]
+            qkv[:, D * i : D * (i + 1)] = total(SHARE + 16 + 16 * i, sources)
+        out[...] = total(SHARE + 64, sources)
+    sums = total(SHARE, range(FRAMES))
+    sums = sums[0:2] + sums[2:4]
+    gain_t[...] = sums[0, :16]
+    gain_s[...] = sums[1, :16]
+    for copy in copies:
+        copy.wait()
 
 
 def unpack(back):
-    def out(*shape):
-        return jax.ShapeDtypeStruct(shape, F32)
-
+    vmem = pl.BlockSpec(memory_space=pltpu.VMEM)
     return pl.pallas_call(
         unpack_kernel,
+        in_specs=[vmem],
+        out_specs=[pl.BlockSpec(memory_space=pl.ANY)] + [vmem] * 6,
         out_shape=(
-            out(1, TOKENS, D), out(16, 3 * D), out(16, D), out(16, 3 * D), out(16, D), out(2, 128)
+            shaped(F32, 1, TOKENS, D),
+            shaped(F32, 16, 3 * D),
+            shaped(F32, 16, D),
+            shaped(F32, 16, 3 * D),
+            shaped(F32, 16, D),
+            shaped(F32, 16),
+            shaped(F32, 16),
         ),
+        scratch_shapes=[pltpu.VMEM((4, 256, D), F32), pltpu.SemaphoreType.DMA((4,))],
+        compiler_params=params(8),
     )(back)
 
 
@@ -387,10 +459,14 @@
 
 
 def per_device(latents, cotangent, gain_time, qkv_time, out_time, gain_space, qkv_space, out_space):
+    gain_time, gain_space = gain_time.reshape(1, D), gain_space.reshape(1, D)
     moved = exchange(pack(latents, cotangent))
-    sent = run_main(moved, gain_time, qkv_time, out_time, gain_space, qkv_space, out_space)
-    *grads, gains = unpack(exchange(sent))
-    return (*grads, gains[0, :16], gains[1, :16])
+    *state, kept, given = run_main(
+        moved, gain_time, qkv_time, out_time, gain_space, qkv_space, out_space
+    )
+    taken = lax.ppermute(given, "frame", [(i, i ^ 1) for i in range(FRAMES)])
+    grads = run_input(*state, gain_time, qkv_time)
+    return tuple(unpack(exchange(join(grads, kept, taken))))
 
 
 def solution(mesh):

time: 76.4 us -> 70.4 us (0.921)
  blocking collectives: 54.2 us -> 47 us
  Pallas kernels: 19.9 us -> 18.6 us
  starting transfers between devices: 0 us -> 1.24 us
  local copies, waits for them, and re-layouts: 1.3 us -> 2.11 us
    all_to_all x2, blocking collectives: 54.2 us -> 47 us  [exchange(): return lax.all_to_all(x, 'frame', split_axis=0, concat_axis=0, tiled=True)]
    unnamed x12 -> x16, local copies, waits for them, and re-layouts: 0.03 us -> 2.11 us
    pallas_call x3 -> x5, Pallas kernels: 19.9 us -> 18.6 us  [the longest x1 14 us: run_main(): pl.pallas_call(main_kernel, out_shape=(shaped(F32, ROWS, D), shaped(BF16,...]
    squeeze x1 -> x0, local copies, waits for them, and re-layouts: 1.28 us -> none  [per_device(): return (*grads, gains[0, :16], gains[1, :16])]
    ppermute x0 -> x1, starting transfers between devices: none -> 1.24 us  [per_device(): taken = lax.ppermute(given, 'frame', [(i, i ^ 1) for i in range(FRAMES)])]
  transfers between devices with their start and end apart: 0 -> 1, of which waited for: 0 -> 1; matrix products, arithmetic and copies ran while one was open for 0% -> 0% of each run, Pallas kernels for 0% -> 2%
where the time goes in v3:
time: 70.4 us; the launch traced here: 70.1 us
  blocking collectives  47 us (67%)
  Pallas kernels  18.6 us (26%)
  local copies, waits for them, and re-layouts  2.11 us (3%)
  starting transfers between devices  1.24 us (2%)
  between operations  0.9 us (1%)
    all_to_all x2, blocking collectives, exchange(): return lax.all_to_all(x, 'frame', split_axis=0, concat_axis=0, tiled=True)  47 us
    pallas_call x1, Pallas kernels, run_main(): pl.pallas_call(main_kernel, out_shape=(shaped(F32, ROWS, D), shaped(BF16,...  14 us
    unnamed x16, local copies, waits for them, and re-layouts  2.11 us
    pallas_call x1, Pallas kernels, unpack(): pl.pallas_call(unpack_kernel, in_specs=[vmem], out_specs=[pl.BlockSpec(me...  1.66 us
    pallas_call x1, Pallas kernels, pack(): pl.pallas_call(pack_kernel, in_specs=[pl.BlockSpec(memory_space=pltpu.HBM...  1.47 us
  transfers between devices with their start and end apart: 1, of which 1 were waited for; matrix products, arithmetic and copies ran while one was open for 0% of the time, Pallas kernels for 2%

profile of v3, /device:TPU:1, one launch (start us, length us, event | category | flops | bytes accessed | tf_op | source)
XLA Modules:
  0.0 70.1 jit_solution(4846831849263924969)
XLA Ops:
  0.6 0.0 copy-start
  0.6 1.0 %copy-done = bf16[1,1024,256]{2,1,0:T(8,128)(2,1)S(1)} copy-done((bf16[1,1024,256]{2,1,0:T(8,128)(2,1)S(1)}, bf16[1,1024,256]{2,1,0:T(8,128)(2,1)}, u32[]{:S(2)}) %copy-start) | copy-done | bytes 524312
  1.7 1.0 %copy-done.1 = bf16[1,1024,256]{2,1,0:T(8,128)(2,1)S(1)} copy-done((bf16[1,1024,256]{2,1,0:T(8,128)(2,1)S(1)}, bf16[1,1024,256]{2,1,0:T(8,128)(2,1)}, u32[]{:S(2)}) %copy-start.1) | copy-done | bytes 524312
  2.7 1.5 %shard_map.135 = bf16[16,128,256]{2,1,0:T(8,128)(2,1)S(1)} custom-call(bf16[1,1024,256]{2,1,0:T(8,128)(2,1)S(1)} %copy-done, bf16[1,1024,256]{2,1,0:T(8,128)(2,1)S(1)} %copy-done.1), custom_call_target="tpu_custom_call" | custom-call | tf_op jit(solution)/shard_map/pallas_call | solution.py:394
  4.2 0.0 copy-start.2
  4.2 0.0 copy-start.3
  4.2 0.0 copy-start.4
  4.2 0.0 copy-start.5
  4.2 0.0 copy-start.6
  4.3 0.0 copy-start.7
  4.3 25.3 %all_to_all.10.moved = bf16[16,128,256]{2,1,0:T(8,128)(2,1)S(1)} all-to-all(bf16[16,128,256]{2,1,0:T(8,128)(2,1)S(1)} %shard_map.135), channel_id=1, replica_groups=mesh['dp'=8,'frame'=16] {'frame'}, dimensions={0} | all-to-all | bytes 2097152 | tf_op jit(solution)/shard_map/all_to_all | solution.py:458
  29.6 0.0 copy-done.2
  29.6 0.0 copy-done.3
  29.6 0.0 copy-done.4
  29.6 0.0 copy-done.5
  29.6 0.0 copy-done.6
  29.6 0.0 copy-done.7
  29.6 14.0 %shard_map.136 = (f32[1024,256]{1,0:T(8,128)S(1)}, bf16[1024,768]{1,0:T(8,128)(2,1)S(1)}, f32[2,1024,128]{2,1,0:T(8,128)S(1)}, f32[1,256]{1,0:T(1,128)S(1)}, bf1...) custom-call(bf16[16,128,256]{2,1,0:T(8,128)(2,1)S(1)} %all_to_all.10.moved, f32[1,256]{1,0:T(1,128)S(1)} %bitcast.3, ...), custom_call_target="tpu_custom_call" | custom-call | flops 8000000000 | bytes 6000000 | tf_op jit(solution)/shard_map/pallas_call | solution.py:323
  43.6 1.2 %collective-permute-start = (bf16[16,64,256]{2,1,0:T(8,128)(2,1)S(1)}, bf16[16,64,256]{2,1,0:T(8,128)(2,1)S(1)}, u32[]{:S(2)}, u32[]{:S(2)}) collective-permute-start(bf16[16,64,256]{2,1,0:T(8,128)(2,1)S(1)} %get-tuple-element.18), channel_id=1, source_target_pairs={{0,1},{1,0},{2,3},{3,2},{4,5},{5,4},{6,7},{7,6},{8,9},{9,8},{10,11... | collective-permute-start | bytes 1572872 | tf_op jit(solution)/shard_map/ppermute | solution.py:467
  44.8 1.3 %shard_map.137.grads = bf16[16,80,256]{2,1,0:T(8,128)(2,1)S(1)} custom-call(f32[1024,256]{1,0:T(8,128)S(1)} %get-tuple-element.13.xs, bf16[1024,768]{1,0:T(8,128)(2,1)S(1)} %get-tuple-element.14.dproj, f32[2,1024,128]{2,1,0:T(8,128)S(1)} %get-tuple-element.15.dmid, f32[1,256]{1,0:T(1,128)S(1)} %get-tuple-element.16.gain_sum_s, f32[1,256]{1,0:T(1,128)S(1)} %bitcast.4, ...), custom_call_target="tpu_custom_call" | custom-call | flops 2000000000 | bytes 6000000 | tf_op jit(solution)/shard_map/pallas_call | solution.py:355
  46.1 0.2 collective-permute-done.taken
  46.4 0.2 shard_map.138
  46.5 21.8 %all_to_all.11.back = bf16[16,144,256]{2,1,0:T(8,128)(2,1)S(1)} all-to-all(bf16[16,144,256]{2,1,0:T(8,128)(2,1)S(1)} %shard_map.138), channel_id=1, replica_groups=mesh['dp'=8,'frame'=16] {'frame'}, dimensions={0} | all-to-all | bytes 2359296 | tf_op jit(solution)/shard_map/all_to_all | solution.py:458
  68.3 1.7 %shard_map.139 = (f32[1,1024,256]{2,1,0:T(8,128)}, f32[16,768]{1,0:T(8,128)}, f32[16,256]{1,0:T(8,128)}, f32[16,768]{1,0:T(8,128)}, f32[16,256]{1,0:T(8,128)}, /*index=5*/f32[16]{0:T(128)}, f32[16]{0:T(128)}) custom-call(bf16[16,144,256]{2,1,0:T(8,128)(2,1)S(1)} %all_to_all.11.back), custom_call_target="tpu_custom_call" | custom-call | tf_op jit(solution)/shard_map/pallas_call | solution.py:439
  (1 shorter events, 0.0 us)
Async XLA Ops:
  0.6 1.0 %copy-start = (bf16[1,1024,256]{2,1,0:T(8,128)(2,1)S(1)}, bf16[1,1024,256]{2,1,0:T(8,128)(2,1)}, u32[]{:S(2)}) copy-start(bf16[1,1024,256]{2,1,0:T(8,128)(2,1)} %latents.1) | copy-start | bytes 1572868
  1.7 1.0 %copy-start.1 = (bf16[1,1024,256]{2,1,0:T(8,128)(2,1)S(1)}, bf16[1,1024,256]{2,1,0:T(8,128)(2,1)}, u32[]{:S(2)}) copy-start(bf16[1,1024,256]{2,1,0:T(8,128)(2,1)} %cotangent.1) | copy-start | bytes 1572868
  4.2 25.4 %copy-start.2 = (bf16[256,768]{1,0:T(8,128)(2,1)S(1)}, bf16[256,768]{1,0:T(8,128)(2,1)}, u32[]{:S(2)}) copy-start(bf16[256,768]{1,0:T(8,128)(2,1)} %qkv_s.1) | copy-start | bytes 1179652
  4.2 25.4 %copy-start.3 = (bf16[256,768]{1,0:T(8,128)(2,1)S(1)}, bf16[256,768]{1,0:T(8,128)(2,1)}, u32[]{:S(2)}) copy-start(bf16[256,768]{1,0:T(8,128)(2,1)} %qkv_t.3) | copy-start | bytes 1179652
  4.2 25.3 %copy-start.4 = (bf16[256,256]{1,0:T(8,128)(2,1)S(1)}, bf16[256,256]{1,0:T(8,128)(2,1)}, u32[]{:S(2)}) copy-start(bf16[256,256]{1,0:T(8,128)(2,1)} %out_t.1) | copy-start | bytes 393220
  4.2 25.3 %copy-start.5 = (bf16[256,256]{1,0:T(8,128)(2,1)S(1)}, bf16[256,256]{1,0:T(8,128)(2,1)}, u32[]{:S(2)}) copy-start(bf16[256,256]{1,0:T(8,128)(2,1)} %out_s.1) | copy-start | bytes 393220
  4.2 25.3 %copy-start.6 = (f32[256]{0:T(256)S(1)}, f32[256]{0:T(256)}, u32[]{:S(2)}) copy-start(f32[256]{0:T(256)} %param.13) | copy-start | bytes 3076
  4.3 25.3 %copy-start.7 = (f32[256]{0:T(256)S(1)}, f32[256]{0:T(256)}, u32[]{:S(2)}) copy-start(f32[256]{0:T(256)} %param.10) | copy-start | bytes 3076
  43.6 2.8 %collective-permute-start = (bf16[16,64,256]{2,1,0:T(8,128)(2,1)S(1)}, bf16[16,64,256]{2,1,0:T(8,128)(2,1)S(1)}, u32[]{:S(2)}, u32[]{:S(2)}) collective-permute-start(bf16[16,64,256]{2,1,0:T(8,128)(2,1)S(1)} %get-tuple-element.18), channel_id=1, source_target_pairs={{0,1},{1,0},{2,3},{3,2},{4,5},{5,4},{6,7},{7,6},{8,9},{9,8},{10,11... | collective-permute-start | bytes 1572872 | tf_op jit(solution)/shard_map/ppermute | solution.py:467

commit v4 on v3

--- a/solution.py
+++ b/solution.py
@@ -40,7 +40,7 @@
 
 
 def head_masks():
-    lane = lax.broadcasted_iota(jnp.int32, (1, HALF), 1) // HEAD_DIM
+    lane = lax.broadcasted_iota(jnp.int32, (1, D), 1) // HEAD_DIM % PACK
     return [(lane == h).astype(F32).astype(BF16) for h in range(PACK)]
 
 
@@ -48,12 +48,41 @@
     return jnp.concatenate([x * m for m in masks], axis=0)
 
 
-def spread_full(x, masks):
-    low, high = spread(x[:, :HALF], masks), spread(x[:, HALF:], masks)
-    zero = jnp.zeros_like(low)
+def halves(x):
+    zero = jnp.zeros((x.shape[0], HALF), x.dtype)
     return jnp.concatenate(
-        [jnp.concatenate([low, zero], axis=1), jnp.concatenate([zero, high], axis=1)], axis=0
+        [
+            jnp.concatenate([x[:, :HALF], zero], axis=1),
+            jnp.concatenate([zero, x[:, HALF:]], axis=1),
+        ],
+        axis=0,
     )
+
+
+def join_halves(x):
+    n = x.shape[0] // 2
+    return jnp.concatenate([x[:n, :HALF], x[n:, HALF:]], axis=1)
+
+
+def each_token(f, x):
+    n = x.shape[0] // 2
+    return jnp.concatenate([f(x[:n]), f(x[n:])], axis=0)
+
+
+def first_token():
+    return lax.broadcasted_iota(jnp.int32, (32, 128), 1) < 64
+
+
+def pair_scores(a, b):
+    both = dot_nt(a, b)
+    return jnp.where(first_token(), both[:32], both[32:])
+
+
+def pair_mix(x, b):
+    zero = jnp.zeros_like(x)
+    one = first_token()
+    both = jnp.concatenate([jnp.where(one, x, zero), jnp.where(one, zero, x)], axis=0)
+    return each_token(join_halves, dot_nn(both.astype(BF16), b))
 
 
 def flip_space(x):
@@ -76,7 +105,7 @@
                 a, b = blocks[i], blocks[i + step]
                 blocks[i] = jnp.where(upper, pltpu.roll(b, 16 * step, 1), a)
                 blocks[i + step] = jnp.where(upper, b, pltpu.roll(a, 128 - 16 * step, 1))
-    return blocks
+    return jnp.concatenate(blocks, axis=0)
 
 
 def softmax_keys(scores, axis):
@@ -141,21 +170,40 @@
 
     lax.fori_loop(0, ROWS // CHUNK, project_time, 0, unroll=True)
 
-    def token(x, s):
-        return x[16 * s : 16 * (s + 1)]
+    def time_pairs(c):
+        return [
+            pl.ds(pl.multiple_of(c * TIME_STEP * GROUP + 32 * i, 32), 32)
+            for i in range(4 * TIME_STEP)
+        ]
+
+    def load(ref, offset, rows):
+        return [ref[r, offset : offset + D] for r in rows]
+
+    def spread_pairs(xs):
+        return [each_token(lambda t: spread(t, masks), x) for x in xs]
+
+    def halves_pairs(xs):
+        return [each_token(halves, x) for x in xs]
+
+    def by_four(xs):
+        return [jnp.concatenate(xs[i : i + 4], axis=0) for i in range(0, len(xs), 4)]
+
+    def in_pairs(xs):
+        return [x[32 * i : 32 * (i + 1)] for x in xs for i in range(4)]
 
     def time_forward(c, _):
-        groups = [rows_of(c * TIME_STEP + i, GROUP) for i in range(TIME_STEP)]
-        q, k, v = ([proj_t[rows, D * i : D * (i + 1)] for rows in groups] for i in range(3))
-        qb = [[spread_full(token(x, s), masks) for s in range(8)] for x in q]
-        scores = [jnp.stack([dot_nt(token(x, s), y[s]) for s in range(8)]) for x, y in zip(k, qb)]
-        probs = [softmax_keys(x, 1).reshape(GROUP, 128) for x in scores]
-        turned = [flip_time(x) for x in probs]
-        vb = [[spread_full(token(x, s), masks) for s in range(8)] for x in v]
-        mixed = [[dot_nn(x[s].astype(BF16), y[s]) for s in range(8)] for x, y in zip(turned, vb)]
-        for n, rows in enumerate(groups):
-            probs_t[rows, :] = probs[n].astype(BF16)
-            mixed_t[rows, :] = jnp.concatenate(mixed[n], axis=0).astype(BF16)
+        rows = time_pairs(c)
+        q, k, v = (load(proj_t, D * i, rows) for i in range(3))
+        qb = spread_pairs(q)
+        scores = by_four([pair_scores(x, y) for x, y in zip(halves_pairs(k), qb)])
+        probs = [softmax_keys(x.reshape(8, 16, 128), 1).reshape(GROUP, 128) for x in scores]
+        turned = in_pairs([flip_time(x) for x in probs])
+        vb = spread_pairs(v)
+        mixed = [pair_mix(x, y) for x, y in zip(turned, vb)]
+        for n in range(TIME_STEP):
+            probs_t[rows_of(c * TIME_STEP + n, GROUP), :] = probs[n].astype(BF16)
+        for r, x in zip(rows, mixed):
+            mixed_t[r, :] = x.astype(BF16)
         return _
 
     lax.fori_loop(0, ROWS // GROUP // TIME_STEP, time_forward, 0)
@@ -182,32 +230,33 @@
     lax.fori_loop(0, ROWS // CHUNK, project_space, 0, unroll=True)
 
     def space(c, _):
-        units = []
-        for i in range(SPACE_STEP):
-            rows = rows_of(c * SPACE_STEP + i, SHARE)
-            units += [(rows, 0), (rows, HALF)]
-
-        def load(ref, offset):
-            return [ref[rows, offset + first : offset + first + HALF] for rows, first in units]
-
-        q, k, v, do = load(proj_s, 0), load(proj_s, D), load(proj_s, 2 * D), load(dmix, 0)
+        rows = [rows_of(c * SPACE_STEP + i, SHARE) for i in range(SPACE_STEP)]
+        q, k, v = (load(proj_s, D * i, rows) for i in range(3))
+        do = load(dmix, 0, rows)
+
+        def split(x):
+            return x.reshape(2, SHARE, D)
+
+        def turn(x):
+            return jnp.concatenate([flip_space(x[:SHARE]), flip_space(x[SHARE:])], axis=0)
+
         qb = [spread(x, masks) for x in q]
-        scores = [dot_nt(x, y) for x, y in zip(k, qb)]
+        scores = [split(dot_nt(halves(x), y)) for x, y in zip(k, qb)]
         dob = [spread(x, masks) for x in do]
-        dprobs = [dot_nt(x, y) for x, y in zip(v, dob)]
-        probs = [softmax_keys(x, 0) for x in scores]
-        probs_b = [x.astype(BF16) for x in probs]
-        ds = [score_grad(x, y, 0).astype(BF16) for x, y in zip(probs, dprobs)]
-        turned = [flip_space(x) for x in probs_b]
-        ds_turned = [flip_space(x) for x in ds]
-        dv = [dot_nn(x, y) for x, y in zip(probs_b, dob)]
-        dk = [dot_nn(x, y) * SCALE for x, y in zip(ds, qb)]
-        mixed = [dot_nn(x, spread(y, masks)) for x, y in zip(turned, v)]
-        dq = [dot_nn(x, spread(y, masks)) * SCALE for x, y in zip(ds_turned, k)]
-        for n, (rows, first) in enumerate(units):
-            mixed_s[rows, first : first + HALF] = mixed[n].astype(BF16)
+        dprobs = [split(dot_nt(halves(x), y)) for x, y in zip(v, dob)]
+        probs = [softmax_keys(x, 1) for x in scores]
+        probs_b = [x.astype(BF16).reshape(2 * SHARE, D) for x in probs]
+        ds = [score_grad(x, y, 1).astype(BF16).reshape(2 * SHARE, D) for x, y in zip(probs, dprobs)]
+        turned = [turn(x) for x in probs_b]
+        ds_turned = [turn(x) for x in ds]
+        dv = [join_halves(dot_nn(x, y)) for x, y in zip(probs_b, dob)]
+        dk = [join_halves(dot_nn(x, y)) * SCALE for x, y in zip(ds, qb)]
+        mixed = [join_halves(dot_nn(x, spread(y, masks))) for x, y in zip(turned, v)]
+        dq = [join_halves(dot_nn(x, spread(y, masks))) * SCALE for x, y in zip(ds_turned, k)]
+        for n, r in enumerate(rows):
+            mixed_s[r, :] = mixed[n].astype(BF16)
             for i, grad in enumerate((dq, dk, dv)):
-                dproj[rows, D * i + first : D * i + first + HALF] = grad[n].astype(BF16)
+                dproj[r, D * i : D * (i + 1)] = grad[n].astype(BF16)
         return _
 
     lax.fori_loop(0, FRAMES // SPACE_STEP, space, 0)
@@ -242,31 +291,24 @@
     lax.fori_loop(0, ROWS // CHUNK, mixed_back, 0, unroll=True)
 
     def time_back(c, _):
-        groups = [rows_of(c * TIME_STEP + i, GROUP) for i in range(TIME_STEP)]
-        q, k, v = ([proj_t[rows, D * i : D * (i + 1)] for rows in groups] for i in range(3))
-        do = [dmix[rows, :] for rows in groups]
-        probs_b = [probs_t[rows, :] for rows in groups]
-        tokens = range(8)
-        dob = [[spread_full(token(x, s), masks) for s in tokens] for x in do]
-        dprobs = [jnp.stack([dot_nt(token(x, s), y[s]) for s in tokens]) for x, y in zip(v, dob)]
+        rows = time_pairs(c)
+        q, k, v = (load(proj_t, D * i, rows) for i in range(3))
+        do = load(dmix, 0, rows)
+        groups = [rows_of(c * TIME_STEP + n, GROUP) for n in range(TIME_STEP)]
+        probs = [probs_t[g, :].astype(F32) for g in groups]
+        dob = spread_pairs(do)
+        dprobs = by_four([pair_scores(x, y) for x, y in zip(halves_pairs(v), dob)])
         ds = [
-            score_grad(x.astype(F32).reshape(8, 16, 128), y, 1).reshape(GROUP, 128)
-            for x, y in zip(probs_b, dprobs)
+            score_grad(x.reshape(8, 16, 128), y.reshape(8, 16, 128), 1).reshape(GROUP, 128)
+            for x, y in zip(probs, dprobs)
         ]
-        turned = [flip_time(x) for x in ds]
-        ds = [x.astype(BF16) for x in ds]
-        dv = [[dot_nn(token(x, s), y[s]) for s in tokens] for x, y in zip(probs_b, dob)]
-        dk = [
-            [dot_nn(token(x, s), spread_full(token(y, s), masks)) * SCALE for s in tokens]
-            for x, y in zip(ds, q)
-        ]
-        dq = [
-            [dot_nn(x[s].astype(BF16), spread_full(token(y, s), masks)) * SCALE for s in tokens]
-            for x, y in zip(turned, k)
-        ]
-        for n, rows in enumerate(groups):
+        turned = in_pairs([flip_time(x) for x in ds])
+        dv = [pair_mix(x, y) for x, y in zip(in_pairs(probs), dob)]
+        dk = [pair_mix(x, y) * SCALE for x, y in zip(in_pairs(ds), spread_pairs(q))]
+        dq = [pair_mix(x, y) * SCALE for x, y in zip(turned, spread_pairs(k))]
+        for n, r in enumerate(rows):
             for i, grad in enumerate((dq, dk, dv)):
-                dproj[rows, D * i : D * (i + 1)] = jnp.concatenate(grad[n], axis=0).astype(BF16)
+                dproj[r, D * i : D * (i + 1)] = grad[n].astype(BF16)
         return _
 
     lax.fori_loop(0, ROWS // GROUP // TIME_STEP, time_back, 0)
@@ -369,37 +411,51 @@
     )(grads, kept, taken)
 
 
-def pack_kernel(latents, cotangent, packed, held, sems):
+def pack_kernel(latents, cotangent, packed, held, ready, sems, out_sems):
     copies = [
-        pltpu.make_async_copy(
-            src.at[0, pl.ds(256 * wy, 256)], held.at[n, wy], sems.at[n, wy]
-        )
+        [
+            pltpu.make_async_copy(src.at[0, pl.ds(256 * wy, 256)], held.at[n, wy], sems.at[n, wy])
+            for n, src in enumerate((latents, cotangent))
+        ]
         for wy in range(4)
-        for n, src in enumerate((latents, cotangent))
     ]
-    for copy in copies:
-        copy.start()
+    for wy in range(4):
+        for copy in copies[wy]:
+            copy.start()
+    outs = []
     for wy in range(4):
         for n in range(2):
-            copies[2 * wy + n].wait()
+            copies[wy][n].wait()
             for pair in range(4):
                 rows = held[n, wy, 64 * pair : 64 * (pair + 1), :].astype(F32).reshape(2, 4, WIN, D)
                 for wx in range(4):
                     both = jnp.concatenate([rows[0, wx], rows[1, wx]], axis=0).astype(BF16)
                     first = SHARE * n + 16 * pair
-                    packed[4 * wy + wx, first : first + 16, :] = both
+                    ready[4 * wy + wx, first : first + 16, :] = both
+        outs.append(
+            pltpu.make_async_copy(
+                ready.at[pl.ds(4 * wy, 4)], packed.at[pl.ds(4 * wy, 4)], out_sems.at[wy]
+            )
+        )
+        outs[wy].start()
+    for copy in outs:
+        copy.wait()
 
 
 def pack(latents, cotangent):
+    anywhere = pl.BlockSpec(memory_space=pl.ANY)
     return pl.pallas_call(
         pack_kernel,
-        in_specs=[pl.BlockSpec(memory_space=pltpu.HBM)] * 2,
+        in_specs=[anywhere] * 2,
+        out_specs=anywhere,
         out_shape=shaped(BF16, FRAMES, 2 * SHARE, D),
         scratch_shapes=[
             pltpu.VMEM((2, 4, 256, D), BF16),
+            pltpu.VMEM((FRAMES, 2 * SHARE, D), BF16),
             pltpu.SemaphoreType.DMA((2, 4)),
+            pltpu.SemaphoreType.DMA((4,)),
         ],
-        compiler_params=params(8),
+        compiler_params=params(60),
     )(latents, cotangent)
 
 

time: 70.4 us -> 67.4 us (0.957)
  local copies, waits for them, and re-layouts: 2.11 us -> 0.04 us
  Pallas kernels: 18.6 us -> 17.7 us
    unnamed x16 -> x12, local copies, waits for them, and re-layouts: 2.11 us -> 0.04 us
    pallas_call x1, Pallas kernels: 14 us -> 12.4 us  [run_main(): pl.pallas_call(main_kernel, out_shape=(shaped(F32, ROWS, D), shaped(BF16,...]
where the time goes in v4:
time: 67.4 us; the launch traced here: 67.1 us
  blocking collectives  47.3 us (70%)
  Pallas kernels  17.7 us (26%)
  starting transfers between devices  1.25 us (2%)
  between operations  0.73 us (1%)
    all_to_all x2, blocking collectives, exchange(): return lax.all_to_all(x, 'frame', split_axis=0, concat_axis=0, tiled=True)  47.3 us
    pallas_call x1, Pallas kernels, run_main(): pl.pallas_call(main_kernel, out_shape=(shaped(F32, ROWS, D), shaped(BF16,...  12.4 us
    pallas_call x1, Pallas kernels, pack(): pl.pallas_call(pack_kernel, in_specs=[anywhere] * 2, out_specs=anywhere,...  2.1 us
    pallas_call x1, Pallas kernels, unpack(): pl.pallas_call(unpack_kernel, in_specs=[vmem], out_specs=[pl.BlockSpec(me...  1.66 us
    pallas_call x1, Pallas kernels, run_input(): pl.pallas_call(input_kernel, out_shape=shaped(BF16, FRAMES, SHARE + 16, D...  1.36 us
  transfers between devices with their start and end apart: 1, of which 1 were waited for; matrix products, arithmetic and copies ran while one was open for 0% of the time, Pallas kernels for 2%

profile of v4, /device:TPU:1, one launch (start us, length us, event | category | flops | bytes accessed | tf_op | source)
XLA Modules:
  0.0 67.1 jit_solution(10594419239727767218)
XLA Ops:
  0.6 2.1 %shard_map.135 = bf16[16,128,256]{2,1,0:T(8,128)(2,1)} custom-call(bf16[1,1024,256]{2,1,0:T(8,128)(2,1)} %latents.1, bf16[1,1024,256]{2,1,0:T(8,128)(2,1)} %cotangent.1), custom_call_target="tpu_custom_call" | custom-call | tf_op jit(solution)/shard_map/pallas_call | solution.py:447
  2.7 0.0 copy-start
  2.8 0.0 copy-start.1
  2.8 0.0 copy-start.2
  2.8 0.0 copy-start.3
  2.8 0.0 copy-start.4
  2.8 0.0 copy-start.5
  2.8 25.5 %all_to_all.10.moved = bf16[16,128,256]{2,1,0:T(8,128)(2,1)S(1)} all-to-all(bf16[16,128,256]{2,1,0:T(8,128)(2,1)} %shard_map.135), channel_id=1, replica_groups=mesh['dp'=8,'frame'=16] {'frame'}, dimensions={0} | all-to-all | bytes 2097152 | tf_op jit(solution)/shard_map/all_to_all | solution.py:514
  28.3 0.0 copy-done
  28.3 0.0 copy-done.1
  28.3 0.0 copy-done.2
  28.3 0.0 copy-done.3
  28.3 0.0 copy-done.4
  28.3 0.0 copy-done.5
  28.4 12.4 %shard_map.136 = (f32[1024,256]{1,0:T(8,128)S(1)}, bf16[1024,768]{1,0:T(8,128)(2,1)S(1)}, f32[2,1024,128]{2,1,0:T(8,128)S(1)}, f32[1,256]{1,0:T(1,128)S(1)}, bf1...) custom-call(bf16[16,128,256]{2,1,0:T(8,128)(2,1)S(1)} %all_to_all.10.moved, f32[1,256]{1,0:T(1,128)S(1)} %bitcast.3, ...), custom_call_target="tpu_custom_call" | custom-call | flops 8000000000 | bytes 6000000 | tf_op jit(solution)/shard_map/pallas_call | solution.py:365
  40.7 1.3 %collective-permute-start = (bf16[16,64,256]{2,1,0:T(8,128)(2,1)S(1)}, bf16[16,64,256]{2,1,0:T(8,128)(2,1)S(1)}, u32[]{:S(2)}, u32[]{:S(2)}) collective-permute-start(bf16[16,64,256]{2,1,0:T(8,128)(2,1)S(1)} %get-tuple-element.18), channel_id=1, source_target_pairs={{0,1},{1,0},{2,3},{3,2},{4,5},{5,4},{6,7},{7,6},{8,9},{9,8},{10,11... | collective-permute-start | bytes 1572872 | tf_op jit(solution)/shard_map/ppermute | solution.py:523
  42.0 1.4 %shard_map.137.grads = bf16[16,80,256]{2,1,0:T(8,128)(2,1)S(1)} custom-call(f32[1024,256]{1,0:T(8,128)S(1)} %get-tuple-element.13.xs, bf16[1024,768]{1,0:T(8,128)(2,1)S(1)} %get-tuple-element.14.dproj, f32[2,1024,128]{2,1,0:T(8,128)S(1)} %get-tuple-element.15.dmid, f32[1,256]{1,0:T(1,128)S(1)} %get-tuple-element.16.gain_sum_s, f32[1,256]{1,0:T(1,128)S(1)} %bitcast.4, ...), custom_call_target="tpu_custom_call" | custom-call | flops 2000000000 | bytes 6000000 | tf_op jit(solution)/shard_map/pallas_call | solution.py:397
  43.3 0.2 collective-permute-done.taken
  43.5 0.2 shard_map.138
  43.7 21.8 %all_to_all.11.back = bf16[16,144,256]{2,1,0:T(8,128)(2,1)S(1)} all-to-all(bf16[16,144,256]{2,1,0:T(8,128)(2,1)S(1)} %shard_map.138), channel_id=1, replica_groups=mesh['dp'=8,'frame'=16] {'frame'}, dimensions={0} | all-to-all | bytes 2359296 | tf_op jit(solution)/shard_map/all_to_all | solution.py:514
  65.4 1.7 %shard_map.139 = (f32[1,1024,256]{2,1,0:T(8,128)}, f32[16,768]{1,0:T(8,128)}, f32[16,256]{1,0:T(8,128)}, f32[16,768]{1,0:T(8,128)}, f32[16,256]{1,0:T(8,128)}, /*index=5*/f32[16]{0:T(128)}, f32[16]{0:T(128)}) custom-call(bf16[16,144,256]{2,1,0:T(8,128)(2,1)S(1)} %all_to_all.11.back), custom_call_target="tpu_custom_call" | custom-call | tf_op jit(solution)/shard_map/pallas_call | solution.py:495
Async XLA Ops:
  2.7 25.6 %copy-start = (bf16[256,768]{1,0:T(8,128)(2,1)S(1)}, bf16[256,768]{1,0:T(8,128)(2,1)}, u32[]{:S(2)}) copy-start(bf16[256,768]{1,0:T(8,128)(2,1)} %qkv_s.1) | copy-start | bytes 1179652
  2.8 25.6 %copy-start.1 = (bf16[256,768]{1,0:T(8,128)(2,1)S(1)}, bf16[256,768]{1,0:T(8,128)(2,1)}, u32[]{:S(2)}) copy-start(bf16[256,768]{1,0:T(8,128)(2,1)} %qkv_t.3) | copy-start | bytes 1179652
  2.8 25.6 %copy-start.2 = (bf16[256,256]{1,0:T(8,128)(2,1)S(1)}, bf16[256,256]{1,0:T(8,128)(2,1)}, u32[]{:S(2)}) copy-start(bf16[256,256]{1,0:T(8,128)(2,1)} %out_t.1) | copy-start | bytes 393220
  2.8 25.5 %copy-start.3 = (bf16[256,256]{1,0:T(8,128)(2,1)S(1)}, bf16[256,256]{1,0:T(8,128)(2,1)}, u32[]{:S(2)}) copy-start(bf16[256,256]{1,0:T(8,128)(2,1)} %out_s.1) | copy-start | bytes 393220
  2.8 25.5 %copy-start.4 = (f32[256]{0:T(256)S(1)}, f32[256]{0:T(256)}, u32[]{:S(2)}) copy-start(f32[256]{0:T(256)} %param.13) | copy-start | bytes 3076
  2.8 25.5 %copy-start.5 = (f32[256]{0:T(256)S(1)}, f32[256]{0:T(256)}, u32[]{:S(2)}) copy-start(f32[256]{0:T(256)} %param.10) | copy-start | bytes 3076
  40.7 2.8 %collective-permute-start = (bf16[16,64,256]{2,1,0:T(8,128)(2,1)S(1)}, bf16[16,64,256]{2,1,0:T(8,128)(2,1)S(1)}, u32[]{:S(2)}, u32[]{:S(2)}) collective-permute-start(bf16[16,64,256]{2,1,0:T(8,128)(2,1)S(1)} %get-tuple-element.18), channel_id=1, source_target_pairs={{0,1},{1,0},{2,3},{3,2},{4,5},{5,4},{6,7},{7,6},{8,9},{9,8},{10,11... | collective-permute-start | bytes 1572872 | tf_op jit(solution)/shard_map/ppermute | solution.py:523

commit v5 on v4

--- a/solution.py
+++ b/solution.py
@@ -18,11 +18,12 @@
 GROUP = 128
 HALF = 128
 PACK = 4
-CHUNK = 512
+CHUNK = 256
 SPACE_STEP = 16
 TIME_STEP = 8
 EPSILON = 1e-06
 SCALE = HEAD_DIM ** (-0.5)
+LOG2E = 1.4426950408889634
 F32 = jnp.float32
 BF16 = jnp.bfloat16
 
@@ -109,8 +110,7 @@
 
 
 def softmax_keys(scores, axis):
-    scores = scores * SCALE
-    ex = jnp.exp(scores - jnp.max(scores, axis=axis, keepdims=True))
+    ex = jnp.exp2((scores - jnp.max(scores, axis=axis, keepdims=True)) * (SCALE * LOG2E))
     return ex * (1.0 / jnp.sum(ex, axis=axis, keepdims=True))
 
 
@@ -132,14 +132,24 @@
     return pl.ds(pl.multiple_of(c * size, size), size)
 
 
-def save(ref, rows, x):
-    for half in range(2):
-        ref[half, rows, :] = x[:, HALF * half : HALF * (half + 1)]
+def swap_matrix():
+    row = lax.broadcasted_iota(jnp.int32, (CHUNK, CHUNK), 0)
+    col = lax.broadcasted_iota(jnp.int32, (CHUNK, CHUNK), 1)
+    return (row == col % 16 * 16 + col // 16).astype(F32).astype(BF16)
+
+
+def block(ref, c, base=0):
+    rows = pl.ds(base + 16 * c, 16)
+    return ref[:, rows, :].reshape(CHUNK, ref.shape[2])
+
+
+def put_block(ref, c, x):
+    ref[:, pl.ds(16 * c, 16), :] = x.reshape(FRAMES, 16, x.shape[1])
 
 
 def main_kernel(
     moved, gain_t, qkv_t, out_t, gain_s, qkv_s, out_s, xs, dproj, dmid, gain_sum_s, kept, given,
-    stage, in_t, proj_t, probs_t, mixed_t, middle, in_s, proj_s, mixed_s, dmix, dmid_b, parts,
+    in_t, proj_t, probs_t, mixed_t, middle, in_s, proj_s, mixed_s, dmix_s, dmix_t, dproj_s, dmid_b, parts,
 ):
     masks = head_masks()
 
@@ -148,27 +158,16 @@
             [ref[half, pl.ds(first, count, stride=stride), :] for half in range(2)], axis=1
         )
 
-    def widen(f, _):
-        save(stage, rows_of(f, SHARE), moved[f, :SHARE, :].astype(F32))
-        return _
-
-    lax.fori_loop(0, FRAMES, widen, 0)
-
-    def by_token(ref, c):
-        return jnp.concatenate([strided(ref, c * (CHUNK // 16) + i, FRAMES, SHARE) for i in range(CHUNK // 16)], axis=0)
-
-    def by_frame(ref, c):
-        return jnp.concatenate([strided(ref, c * (CHUNK // SHARE) + i, SHARE, FRAMES) for i in range(CHUNK // SHARE)], axis=0)
-
-    def project_time(c, _):
-        x = by_token(stage, c)
-        xs[rows_of(c), :] = x
-        inp = (x * norm_factor(x) * gain_t[...]).astype(BF16)
-        in_t[rows_of(c), :] = inp
-        proj_t[rows_of(c), :] = dot_nn(inp, qkv_t[...]).astype(BF16)
-        return _
-
-    lax.fori_loop(0, ROWS // CHUNK, project_time, 0, unroll=True)
+    swap = swap_matrix()
+
+    chunks = range(ROWS // CHUNK)
+    x = [dot_nn(swap, block(moved, c)) for c in chunks]
+    inp = [(y * norm_factor(y) * gain_t[...]).astype(BF16) for y in x]
+    proj = [dot_nn(y, qkv_t[...]).astype(BF16) for y in inp]
+    for c in chunks:
+        xs[rows_of(c), :] = x[c].astype(BF16)
+        in_t[rows_of(c), :] = inp[c]
+        proj_t[rows_of(c), :] = proj[c]
 
     def time_pairs(c):
         return [
@@ -208,31 +207,21 @@
 
     lax.fori_loop(0, ROWS // GROUP // TIME_STEP, time_forward, 0)
 
-    def make_middle(c, _):
-        mid = xs[rows_of(c), :] + dot_nn(mixed_t[rows_of(c), :], out_t[...])
-        save(stage, rows_of(c), mid.astype(BF16).astype(F32))
-        return _
-
-    lax.fori_loop(0, ROWS // CHUNK, make_middle, 0, unroll=True)
-
-    def cots(c):
-        return moved[pl.ds(CHUNK // SHARE * c, CHUNK // SHARE), SHARE:, :].reshape(CHUNK, D)
-
-    def project_space(c, _):
-        mid = by_frame(stage, c)
-        middle[rows_of(c), :] = mid
-        inp = (mid * norm_factor(mid) * gain_s[...]).astype(BF16)
-        in_s[rows_of(c), :] = inp
-        proj_s[rows_of(c), :] = dot_nn(inp, qkv_s[...]).astype(BF16)
-        dmix[rows_of(c), :] = dot_nt(cots(c), out_s[...]).astype(BF16)
-        return _
-
-    lax.fori_loop(0, ROWS // CHUNK, project_space, 0, unroll=True)
+    dmix = [dot_nt(block(moved, c, SHARE), out_s[...]).astype(BF16) for c in chunks]
+    mid = [xs[rows_of(c), :].astype(F32) + dot_nn(mixed_t[rows_of(c), :], out_t[...]) for c in chunks]
+    mid = [dot_nn(swap, y.astype(BF16)) for y in mid]
+    inp = [(y * norm_factor(y) * gain_s[...]).astype(BF16) for y in mid]
+    proj = [dot_nn(y, qkv_s[...]).astype(BF16) for y in inp]
+    for c in chunks:
+        put_block(dmix_s, c, dmix[c])
+        put_block(middle, c, mid[c])
+        put_block(in_s, c, inp[c])
+        put_block(proj_s, c, proj[c])
 
     def space(c, _):
-        rows = [rows_of(c * SPACE_STEP + i, SHARE) for i in range(SPACE_STEP)]
-        q, k, v = (load(proj_s, D * i, rows) for i in range(3))
-        do = load(dmix, 0, rows)
+        rows = [c * SPACE_STEP + i for i in range(SPACE_STEP)]
+        q, k, v = ([proj_s[r, :, D * i : D * (i + 1)] for r in rows] for i in range(3))
+        do = [dmix_s[r] for r in rows]
 
         def split(x):
             return x.reshape(2, SHARE, D)
@@ -254,9 +243,9 @@
         mixed = [join_halves(dot_nn(x, spread(y, masks))) for x, y in zip(turned, v)]
         dq = [join_halves(dot_nn(x, spread(y, masks))) * SCALE for x, y in zip(ds_turned, k)]
         for n, r in enumerate(rows):
-            mixed_s[r, :] = mixed[n].astype(BF16)
+            mixed_s[r] = mixed[n].astype(BF16)
             for i, grad in enumerate((dq, dk, dv)):
-                dproj[r, D * i : D * (i + 1)] = grad[n].astype(BF16)
+                dproj_s[r, :, D * i : D * (i + 1)] = grad[n].astype(BF16)
         return _
 
     lax.fori_loop(0, FRAMES // SPACE_STEP, space, 0)
@@ -269,31 +258,32 @@
                     16 * d : 16 * (d + 1), D * i : D * (i + 1)
                 ]
 
-    place(1, 0, dot_tn(in_s[...], dproj[...]))
-    place(1, 48, dot_tn(mixed_s[...], moved[:, SHARE:, :].reshape(ROWS, D)))
-
-    def middle_back(c, gain_sum):
-        dinput = dot_nt(dproj[rows_of(c), :], qkv_s[...])
-        mid = middle[rows_of(c), :]
-        factor = norm_factor(mid)
-        normed = mid * factor
-        save(dmid, rows_of(c), cots(c).astype(F32) + norm_back(dinput, normed, factor, gain_s[...]))
-        return gain_sum + jnp.sum(dinput * normed, axis=0, keepdims=True)
-
-    gain_sum_s[...] = lax.fori_loop(0, ROWS // CHUNK, middle_back, jnp.zeros((1, D), F32), unroll=True)
-
-    def mixed_back(c, _):
-        dm = by_token(dmid, c).astype(BF16)
-        dmid_b[rows_of(c), :] = dm
-        dmix[rows_of(c), :] = dot_nt(dm, out_t[...]).astype(BF16)
-        return _
-
-    lax.fori_loop(0, ROWS // CHUNK, mixed_back, 0, unroll=True)
+    def flat(ref):
+        return ref[...].reshape(ROWS, ref.shape[2])
+
+    place(1, 0, dot_tn(flat(in_s), flat(dproj_s)))
+    place(1, 48, dot_tn(flat(mixed_s), moved[:, SHARE:, :].reshape(ROWS, D)))
+
+    dinput = [dot_nt(block(dproj_s, c), qkv_s[...]) for c in chunks]
+    mid = [block(middle, c) for c in chunks]
+    factor = [norm_factor(y) for y in mid]
+    normed = [y * f for y, f in zip(mid, factor)]
+    dnorm = [norm_back(d, n, f, gain_s[...]) for d, n, f in zip(dinput, normed, factor)]
+    dm = [block(moved, c, SHARE).astype(F32) + dnorm[c] for c in chunks]
+    dm_b = [dot_nn(swap, y.astype(BF16)).astype(BF16) for y in dm]
+    dmix = [dot_nt(y, out_t[...]).astype(BF16) for y in dm_b]
+    for c in chunks:
+        put_block(dmid, c, dm[c])
+        dmid_b[rows_of(c), :] = dm_b[c]
+        dmix_t[rows_of(c), :] = dmix[c]
+    gain_sum_s[...] = sum(
+        jnp.sum(d * n, axis=0, keepdims=True) for d, n in zip(dinput, normed)
+    )
 
     def time_back(c, _):
         rows = time_pairs(c)
         q, k, v = (load(proj_t, D * i, rows) for i in range(3))
-        do = load(dmix, 0, rows)
+        do = load(dmix_t, 0, rows)
         groups = [rows_of(c * TIME_STEP + n, GROUP) for n in range(TIME_STEP)]
         probs = [probs_t[g, :].astype(F32) for g in groups]
         dob = spread_pairs(do)
@@ -321,16 +311,18 @@
     given[...] = parts[1 - core]
 
 
-def input_kernel(xs, dproj, dmid, gain_sum_s, gain_t, qkv_t, sent, stage):
-    def input_back(c, gain_sum):
-        dinput = dot_nt(dproj[rows_of(c), :], qkv_t[...])
-        x = xs[rows_of(c), :]
-        factor = norm_factor(x)
-        normed = x * factor
-        save(stage, rows_of(c), norm_back(dinput, normed, factor, gain_t[...]))
-        return gain_sum + jnp.sum(dinput * normed, axis=0, keepdims=True)
-
-    gain_sum_t = lax.fori_loop(0, ROWS // CHUNK, input_back, jnp.zeros((1, D), F32), unroll=True)
+def input_kernel(xs, dproj, dmid, gain_sum_s, gain_t, qkv_t, sent):
+    swap = swap_matrix()
+    chunks = range(ROWS // CHUNK)
+    dinput = [dot_nt(dproj[rows_of(c), :], qkv_t[...]) for c in chunks]
+    x = [xs[rows_of(c), :].astype(F32) for c in chunks]
+    factor = [norm_factor(y) for y in x]
+    normed = [y * f for y, f in zip(x, factor)]
+    dnorm = [norm_back(d, n, f, gain_t[...]) for d, n, f in zip(dinput, normed, factor)]
+    dnorm = [dot_nn(swap, y.astype(BF16)) for y in dnorm]
+    for c in chunks:
+        put_block(sent, c, (block(dmid, c) + dnorm[c]).astype(BF16))
+    gain_sum_t = sum(jnp.sum(d * n, axis=0, keepdims=True) for d, n in zip(dinput, normed))
 
     gains = jnp.concatenate([gain_sum_t, gain_sum_s[...]], axis=0)
     high = gains.astype(BF16).astype(F32)
@@ -339,10 +331,6 @@
     for f in range(FRAMES):
         turned = extra if f == 0 else pltpu.roll(extra, D - 16 * f, 1)
         sent[f, SHARE:, :] = turned.astype(BF16)
-        for half in range(2):
-            dnorm = stage[half, pl.ds(f, SHARE, stride=FRAMES), :]
-            total = dmid[half, SHARE * f : SHARE * (f + 1), :] + dnorm
-            sent[f, :SHARE, HALF * half : HALF * (half + 1)] = total.astype(BF16)
 
 
 def join_kernel(grads, kept, taken, sent):
@@ -362,27 +350,31 @@
     def rows(width, kind):
         return pltpu.VMEM((ROWS, width), kind)
 
+    def frames(width, kind):
+        return pltpu.VMEM((FRAMES, SHARE, width), kind)
+
     return pl.pallas_call(
         main_kernel,
         out_shape=(
-            shaped(F32, ROWS, D),
+            shaped(BF16, ROWS, D),
             shaped(BF16, ROWS, 3 * D),
-            shaped(F32, 2, ROWS, HALF),
+            shaped(F32, FRAMES, SHARE, D),
             shaped(F32, 1, D),
             shaped(BF16, FRAMES, SHARE, D),
             shaped(BF16, FRAMES, SHARE, D),
         ),
         scratch_shapes=[
-            pltpu.VMEM((2, ROWS, HALF), F32),
             rows(D, BF16),
             rows(3 * D, BF16),
             rows(128, BF16),
             rows(D, BF16),
-            rows(D, F32),
+            frames(D, F32),
+            frames(D, BF16),
+            frames(3 * D, BF16),
+            frames(D, BF16),
+            frames(D, BF16),
             rows(D, BF16),
-            rows(3 * D, BF16),
-            rows(D, BF16),
-            rows(D, BF16),
+            frames(3 * D, BF16),
             rows(D, BF16),
             pltpu.VMEM((2, FRAMES, SHARE, D), BF16),
         ],
@@ -397,7 +389,6 @@
     return pl.pallas_call(
         input_kernel,
         out_shape=shaped(BF16, FRAMES, SHARE + 16, D),
-        scratch_shapes=[pltpu.VMEM((2, ROWS, HALF), F32)],
         compiler_params=params(16),
         cost_estimate=pl.CostEstimate(flops=2 * 10**9, bytes_accessed=6 * 10**6, transcendentals=0),
     )(xs, dproj, dmid, gain_sum_s, gain_t, qkv_t)

time: 67.4 us -> 65.6 us (0.973)
  Pallas kernels: 17.7 us -> 15.6 us
    pallas_call x1, Pallas kernels: 12.4 us -> 10.6 us  [run_main(): pl.pallas_call(main_kernel, out_shape=(shaped(BF16, ROWS, D), shaped(BF16...]
where the time goes in v5:
time: 65.6 us; the launch traced here: 65.4 us
  blocking collectives  47.3 us (72%)
  Pallas kernels  15.6 us (24%)
  starting transfers between devices  1.26 us (2%)
  between operations  0.73 us (1%)
    all_to_all x2, blocking collectives, exchange(): return lax.all_to_all(x, 'frame', split_axis=0, concat_axis=0, tiled=True)  47.3 us
    pallas_call x1, Pallas kernels, run_main(): pl.pallas_call(main_kernel, out_shape=(shaped(BF16, ROWS, D), shaped(BF16...  10.6 us
    pallas_call x1, Pallas kernels, pack(): pl.pallas_call(pack_kernel, in_specs=[anywhere] * 2, out_specs=anywhere,...  2.1 us
    pallas_call x1, Pallas kernels, unpack(): pl.pallas_call(unpack_kernel, in_specs=[vmem], out_specs=[pl.BlockSpec(me...  1.66 us
  transfers between devices with their start and end apart: 1, of which 1 were waited for; matrix products, arithmetic and copies ran while one was open for 0% of the time, Pallas kernels for 2%

profile of v5, /device:TPU:1, one launch (start us, length us, event | category | flops | bytes accessed | tf_op | source)
XLA Modules:
  0.0 65.4 jit_solution(13396268098770863811)
XLA Ops:
  0.6 2.1 %shard_map.135 = bf16[16,128,256]{2,1,0:T(8,128)(2,1)} custom-call(bf16[1,1024,256]{2,1,0:T(8,128)(2,1)} %latents.1, bf16[1,1024,256]{2,1,0:T(8,128)(2,1)} %cotangent.1), custom_call_target="tpu_custom_call" | custom-call | tf_op jit(solution)/shard_map/pallas_call | solution.py:438
  2.7 0.0 copy-start
  2.8 0.0 copy-start.1
  2.8 0.0 copy-start.2
  2.8 0.0 copy-start.3
  2.8 0.0 copy-start.4
  2.8 0.0 copy-start.5
  2.8 25.5 %all_to_all.10.moved = bf16[16,128,256]{2,1,0:T(8,128)(2,1)S(1)} all-to-all(bf16[16,128,256]{2,1,0:T(8,128)(2,1)} %shard_map.135), channel_id=1, replica_groups=mesh['dp'=8,'frame'=16] {'frame'}, dimensions={0} | all-to-all | bytes 2097152 | tf_op jit(solution)/shard_map/all_to_all | solution.py:505
  28.3 0.0 copy-done
  28.3 0.0 copy-done.1
  28.3 0.0 copy-done.2
  28.3 0.0 copy-done.3
  28.3 0.0 copy-done.4
  28.3 0.0 copy-done.5
  28.4 10.6 %shard_map.136 = (bf16[1024,256]{1,0:T(8,128)(2,1)S(1)}, bf16[1024,768]{1,0:T(8,128)(2,1)S(1)}, f32[16,64,256]{2,1,0:T(8,128)S(1)}, f32[1,256]{1,0:T(1,128)S(1)}...) custom-call(bf16[16,128,256]{2,1,0:T(8,128)(2,1)S(1)} %all_to_all.10.moved, f32[1,256]{1,0:T(1,128)S(1)} %bitcast.3, ...), custom_call_target="tpu_custom_call" | custom-call | flops 8000000000 | bytes 6000000 | tf_op jit(solution)/shard_map/pallas_call | solution.py:356
  39.0 1.3 %collective-permute-start = (bf16[16,64,256]{2,1,0:T(8,128)(2,1)S(1)}, bf16[16,64,256]{2,1,0:T(8,128)(2,1)S(1)}, u32[]{:S(2)}, u32[]{:S(2)}) collective-permute-start(bf16[16,64,256]{2,1,0:T(8,128)(2,1)S(1)} %get-tuple-element.18), channel_id=1, source_target_pairs={{0,1},{1,0},{2,3},{3,2},{4,5},{5,4},{6,7},{7,6},{8,9},{9,8},{10,11... | collective-permute-start | bytes 1572872 | tf_op jit(solution)/shard_map/ppermute | solution.py:514
  40.2 1.0 %shard_map.137.grads = bf16[16,80,256]{2,1,0:T(8,128)(2,1)S(1)} custom-call(bf16[1024,256]{1,0:T(8,128)(2,1)S(1)} %get-tuple-element.13.xs, bf16[1024,768]{1,0:T(8,128)(2,1)S(1)} %get-tuple-element.14.dproj, f32[16,64,256]{2,1,0:T(8,128)S(1)} %get-tuple-element.15.dmid, f32[1,256]{1,0:T(1,128)S(1)} %get-tuple-element.16.gain_sum_s, f32[1,256]{1,0:T(1,128)S(1)} %bitcast.4, ...), custom_call_target="tpu_custom_call" | custom-call | flops 2000000000 | bytes 6000000 | tf_op jit(solution)/shard_map/pallas_call | solution.py:389
  41.2 0.5 collective-permute-done.taken
  41.8 0.2 shard_map.138
  41.9 21.8 %all_to_all.11.back = bf16[16,144,256]{2,1,0:T(8,128)(2,1)S(1)} all-to-all(bf16[16,144,256]{2,1,0:T(8,128)(2,1)S(1)} %shard_map.138), channel_id=1, replica_groups=mesh['dp'=8,'frame'=16] {'frame'}, dimensions={0} | all-to-all | bytes 2359296 | tf_op jit(solution)/shard_map/all_to_all | solution.py:505
  63.7 1.7 %shard_map.139 = (f32[1,1024,256]{2,1,0:T(8,128)}, f32[16,768]{1,0:T(8,128)}, f32[16,256]{1,0:T(8,128)}, f32[16,768]{1,0:T(8,128)}, f32[16,256]{1,0:T(8,128)}, /*index=5*/f32[16]{0:T(128)}, f32[16]{0:T(128)}) custom-call(bf16[16,144,256]{2,1,0:T(8,128)(2,1)S(1)} %all_to_all.11.back), custom_call_target="tpu_custom_call" | custom-call | tf_op jit(solution)/shard_map/pallas_call | solution.py:486
Async XLA Ops:
  2.7 25.6 %copy-start = (bf16[256,768]{1,0:T(8,128)(2,1)S(1)}, bf16[256,768]{1,0:T(8,128)(2,1)}, u32[]{:S(2)}) copy-start(bf16[256,768]{1,0:T(8,128)(2,1)} %qkv_s.1) | copy-start | bytes 1179652
  2.8 25.6 %copy-start.1 = (bf16[256,768]{1,0:T(8,128)(2,1)S(1)}, bf16[256,768]{1,0:T(8,128)(2,1)}, u32[]{:S(2)}) copy-start(bf16[256,768]{1,0:T(8,128)(2,1)} %qkv_t.3) | copy-start | bytes 1179652
  2.8 25.6 %copy-start.2 = (bf16[256,256]{1,0:T(8,128)(2,1)S(1)}, bf16[256,256]{1,0:T(8,128)(2,1)}, u32[]{:S(2)}) copy-start(bf16[256,256]{1,0:T(8,128)(2,1)} %out_t.1) | copy-start | bytes 393220
  2.8 25.5 %copy-start.3 = (bf16[256,256]{1,0:T(8,128)(2,1)S(1)}, bf16[256,256]{1,0:T(8,128)(2,1)}, u32[]{:S(2)}) copy-start(bf16[256,256]{1,0:T(8,128)(2,1)} %out_s.1) | copy-start | bytes 393220
  2.8 25.5 %copy-start.4 = (f32[256]{0:T(256)S(1)}, f32[256]{0:T(256)}, u32[]{:S(2)}) copy-start(f32[256]{0:T(256)} %param.13) | copy-start | bytes 3076
  2.8 25.5 %copy-start.5 = (f32[256]{0:T(256)S(1)}, f32[256]{0:T(256)}, u32[]{:S(2)}) copy-start(f32[256]{0:T(256)} %param.10) | copy-start | bytes 3076
  39.0 2.8 %collective-permute-start = (bf16[16,64,256]{2,1,0:T(8,128)(2,1)S(1)}, bf16[16,64,256]{2,1,0:T(8,128)(2,1)S(1)}, u32[]{:S(2)}, u32[]{:S(2)}) collective-permute-start(bf16[16,64,256]{2,1,0:T(8,128)(2,1)S(1)} %get-tuple-element.18), channel_id=1, source_target_pairs={{0,1},{1,0},{2,3},{3,2},{4,5},{5,4},{6,7},{7,6},{8,9},{9,8},{10,11... | collective-permute-start | bytes 1572872 | tf_op jit(solution)/shard_map/ppermute | solution.py:514

commit v6 on v5

--- a/solution.py
+++ b/solution.py
@@ -148,7 +148,7 @@
 
 
 def main_kernel(
-    moved, gain_t, qkv_t, out_t, gain_s, qkv_s, out_s, xs, dproj, dmid, gain_sum_s, kept, given,
+    moved, gain_t, qkv_t, out_t, gain_s, qkv_s, out_s, xs, dproj, dmid, kept, given,
     in_t, proj_t, probs_t, mixed_t, middle, in_s, proj_s, mixed_s, dmix_s, dmix_t, dproj_s, dmid_b, parts,
 ):
     masks = head_masks()
@@ -276,9 +276,6 @@
         put_block(dmid, c, dm[c])
         dmid_b[rows_of(c), :] = dm_b[c]
         dmix_t[rows_of(c), :] = dmix[c]
-    gain_sum_s[...] = sum(
-        jnp.sum(d * n, axis=0, keepdims=True) for d, n in zip(dinput, normed)
-    )
 
     def time_back(c, _):
         rows = time_pairs(c)
@@ -311,7 +308,7 @@
     given[...] = parts[1 - core]
 
 
-def input_kernel(xs, dproj, dmid, gain_sum_s, gain_t, qkv_t, sent):
+def input_kernel(xs, dproj, dmid, gain_t, qkv_t, sent):
     swap = swap_matrix()
     chunks = range(ROWS // CHUNK)
     dinput = [dot_nt(dproj[rows_of(c), :], qkv_t[...]) for c in chunks]
@@ -322,20 +319,11 @@
     dnorm = [dot_nn(swap, y.astype(BF16)) for y in dnorm]
     for c in chunks:
         put_block(sent, c, (block(dmid, c) + dnorm[c]).astype(BF16))
-    gain_sum_t = sum(jnp.sum(d * n, axis=0, keepdims=True) for d, n in zip(dinput, normed))
-
-    gains = jnp.concatenate([gain_sum_t, gain_sum_s[...]], axis=0)
-    high = gains.astype(BF16).astype(F32)
-    low = gains - high
-    extra = jnp.concatenate([high, low, jnp.zeros((12, D), F32)], axis=0)
-    for f in range(FRAMES):
-        turned = extra if f == 0 else pltpu.roll(extra, D - 16 * f, 1)
-        sent[f, SHARE:, :] = turned.astype(BF16)
 
 
 def join_kernel(grads, kept, taken, sent):
-    sent[:, : SHARE + 16, :] = grads[...]
-    sent[:, SHARE + 16 :, :] = (kept[...].astype(F32) + taken[...].astype(F32)).astype(BF16)
+    sent[:, :SHARE, :] = grads[...]
+    sent[:, SHARE:, :] = (kept[...].astype(F32) + taken[...].astype(F32)).astype(BF16)
 
 
 def shaped(kind, *shape):
@@ -359,7 +347,6 @@
             shaped(BF16, ROWS, D),
             shaped(BF16, ROWS, 3 * D),
             shaped(F32, FRAMES, SHARE, D),
-            shaped(F32, 1, D),
             shaped(BF16, FRAMES, SHARE, D),
             shaped(BF16, FRAMES, SHARE, D),
         ),
@@ -385,19 +372,19 @@
     )(moved, gain_t, qkv_t, out_t, gain_s, qkv_s, out_s)
 
 
-def run_input(xs, dproj, dmid, gain_sum_s, gain_t, qkv_t):
+def run_input(xs, dproj, dmid, gain_t, qkv_t):
     return pl.pallas_call(
         input_kernel,
-        out_shape=shaped(BF16, FRAMES, SHARE + 16, D),
+        out_shape=shaped(BF16, FRAMES, SHARE, D),
         compiler_params=params(16),
         cost_estimate=pl.CostEstimate(flops=2 * 10**9, bytes_accessed=6 * 10**6, transcendentals=0),
-    )(xs, dproj, dmid, gain_sum_s, gain_t, qkv_t)
+    )(xs, dproj, dmid, gain_t, qkv_t)
 
 
 def join(grads, kept, taken):
     return pl.pallas_call(
         join_kernel,
-        out_shape=shaped(BF16, FRAMES, 2 * SHARE + 16, D),
+        out_shape=shaped(BF16, FRAMES, 2 * SHARE, D),
         compiler_params=params(8),
     )(grads, kept, taken)
 
@@ -450,7 +437,18 @@
     )(latents, cotangent)
 
 
-def unpack_kernel(back, grads, qkv_t, out_t, qkv_s, out_s, gain_t, gain_s, held, sems):
+def gain_sums(sums, weights, gain, me):
+    own = weights[pl.ds(pl.multiple_of(16 * me, 16), 16), :].astype(F32)
+    column = jnp.sum(own * sums, axis=-1, keepdims=True)
+    row = jnp.broadcast_to(column, (16, 128)).T[:1, :]
+    turned = pltpu.roll(jnp.broadcast_to(gain[...], (8, D)), (D - 16 * me) % D, 1)
+    return row / turned[:1, :16]
+
+
+def unpack_kernel(
+    back, gains_t, weights_t, gains_s, weights_s,
+    grads, qkv_t, out_t, qkv_s, out_s, gain_t, gain_s, held, sems,
+):
     copies = []
     for wy in range(4):
         for pair in range(4):
@@ -468,24 +466,25 @@
     def total(first, sources):
         return sum(back[f, first : first + 16, :].astype(F32) for f in sources) * inverse
 
-    for core, qkv, out in ((0, qkv_t, out_t), (1, qkv_s, out_s)):
+    me = lax.axis_index("frame")
+    for core, qkv, out, gain, weights, gain_out in (
+        (0, qkv_t, out_t, gains_t, weights_t, gain_t),
+        (1, qkv_s, out_s, gains_s, weights_s, gain_s),
+    ):
         sources = range(core, FRAMES, 2)
-        for i in range(3):
-            qkv[:, D * i : D * (i + 1)] = total(SHARE + 16 + 16 * i, sources)
-        out[...] = total(SHARE + 64, sources)
-    sums = total(SHARE, range(FRAMES))
-    sums = sums[0:2] + sums[2:4]
-    gain_t[...] = sums[0, :16]
-    gain_s[...] = sums[1, :16]
+        sums = jnp.concatenate([total(SHARE + 16 * i, sources) for i in range(3)], axis=1)
+        qkv[...] = sums
+        out[...] = total(SHARE + 48, sources)
+        gain_out[...] = gain_sums(sums, weights, gain, me)[0]
     for copy in copies:
         copy.wait()
 
 
-def unpack(back):
+def unpack(back, gain_t, qkv_t, gain_s, qkv_s):
     vmem = pl.BlockSpec(memory_space=pltpu.VMEM)
     return pl.pallas_call(
         unpack_kernel,
-        in_specs=[vmem],
+        in_specs=[vmem] * 5,
         out_specs=[pl.BlockSpec(memory_space=pl.ANY)] + [vmem] * 6,
         out_shape=(
             shaped(F32, 1, TOKENS, D),
@@ -498,7 +497,7 @@
         ),
         scratch_shapes=[pltpu.VMEM((4, 256, D), F32), pltpu.SemaphoreType.DMA((4,))],
         compiler_params=params(8),
-    )(back)
+    )(back, gain_t, qkv_t, gain_s, qkv_s)
 
 
 def exchange(x):
@@ -513,7 +512,8 @@
     )
     taken = lax.ppermute(given, "frame", [(i, i ^ 1) for i in range(FRAMES)])
     grads = run_input(*state, gain_time, qkv_time)
-    return tuple(unpack(exchange(join(grads, kept, taken))))
+    back = exchange(join(grads, kept, taken))
+    return tuple(unpack(back, gain_time, qkv_time, gain_space, qkv_space))
 
 
 def solution(mesh):

time: 65.6 us -> 63.7 us (0.971)
  blocking collectives: 47.3 us -> 45.3 us
    all_to_all x2, blocking collectives: 47.3 us -> 45.3 us  [exchange(): return lax.all_to_all(x, 'frame', split_axis=0, concat_axis=0, tiled=True)]
where the time goes in v6:
time: 63.7 us; the launch traced here: 63.5 us
  blocking collectives  45.3 us (71%)
  Pallas kernels  15.6 us (24%)
  starting transfers between devices  1.25 us (2%)
  between operations  0.73 us (1%)
    all_to_all x2, blocking collectives, exchange(): return lax.all_to_all(x, 'frame', split_axis=0, concat_axis=0, tiled=True)  45.3 us
    pallas_call x1, Pallas kernels, run_main(): pl.pallas_call(main_kernel, out_shape=(shaped(BF16, ROWS, D), shaped(BF16...  10.6 us
    pallas_call x1, Pallas kernels, pack(): pl.pallas_call(pack_kernel, in_specs=[anywhere] * 2, out_specs=anywhere,...  2.1 us
    pallas_call x1, Pallas kernels, unpack(): pl.pallas_call(unpack_kernel, in_specs=[vmem] * 5, out_specs=[pl.BlockSpe...  1.78 us
  transfers between devices with their start and end apart: 1, of which 1 were waited for; matrix products, arithmetic and copies ran while one was open for 0% of the time, Pallas kernels for 2%

profile of v6, /device:TPU:1, one launch (start us, length us, event | category | flops | bytes accessed | tf_op | source)
XLA Modules:
  0.0 63.5 jit_solution(4080963531798997568)
XLA Ops:
  0.6 2.1 %shard_map.135 = bf16[16,128,256]{2,1,0:T(8,128)(2,1)} custom-call(bf16[1,1024,256]{2,1,0:T(8,128)(2,1)} %latents.1, bf16[1,1024,256]{2,1,0:T(8,128)(2,1)} %cotangent.1), custom_call_target="tpu_custom_call" | custom-call | tf_op jit(solution)/shard_map/pallas_call | solution.py:425
  2.7 0.0 copy-start
  2.8 0.0 copy-start.1
  2.8 0.0 copy-start.2
  2.8 0.0 copy-start.3
  2.8 0.0 copy-start.4
  2.8 0.0 copy-start.5
  2.8 25.5 %all_to_all.10.moved = bf16[16,128,256]{2,1,0:T(8,128)(2,1)S(1)} all-to-all(bf16[16,128,256]{2,1,0:T(8,128)(2,1)} %shard_map.135), channel_id=1, replica_groups=mesh['dp'=8,'frame'=16] {'frame'}, dimensions={0} | all-to-all | bytes 2097152 | tf_op jit(solution)/shard_map/all_to_all | solution.py:504
  28.3 0.0 copy-done
  28.3 0.0 copy-done.1
  28.3 0.0 copy-done.2
  28.3 0.0 copy-done.3
  28.3 0.0 copy-done.4
  28.3 0.0 copy-done.5
  28.4 10.6 %shard_map.136 = (bf16[1024,256]{1,0:T(8,128)(2,1)S(1)}, bf16[1024,768]{1,0:T(8,128)(2,1)S(1)}, f32[16,64,256]{2,1,0:T(8,128)S(1)}, bf16[16,64,256]{2,1,0:T(8,128)(2,1)S(1)}, bf16[16,64,256]{2,1,0:T(8,128)(2,1)S(1)}) custom-call(bf16[16,128,256]{2,1,0:T(8,128)(2,1)S(1)} %all_to_all.10.moved, f32[1,256]{1,0:T(1,128)S(1)} %bitcast.2, ...), custom_call_target="tpu_custom_call" | custom-call | flops 8000000000 | bytes 6000000 | tf_op jit(solution)/shard_map/pallas_call | solution.py:344
  38.9 1.2 %collective-permute-start = (bf16[16,64,256]{2,1,0:T(8,128)(2,1)S(1)}, bf16[16,64,256]{2,1,0:T(8,128)(2,1)S(1)}, u32[]{:S(2)}, u32[]{:S(2)}) collective-permute-start(bf16[16,64,256]{2,1,0:T(8,128)(2,1)S(1)} %get-tuple-element.16), channel_id=1, source_target_pairs={{0,1},{1,0},{2,3},{3,2},{4,5},{5,4},{6,7},{7,6},{8,9},{9,8},{10,11... | collective-permute-start | bytes 1572872 | tf_op jit(solution)/shard_map/ppermute | solution.py:513
  40.2 1.0 %shard_map.137.grads = bf16[16,64,256]{2,1,0:T(8,128)(2,1)S(1)} custom-call(bf16[1024,256]{1,0:T(8,128)(2,1)S(1)} %get-tuple-element.12.xs, bf16[1024,768]{1,0:T(8,128)(2,1)S(1)} %get-tuple-element.13.dproj, f32[16,64,256]{2,1,0:T(8,128)S(1)} %get-tuple-element.14.dmid, f32[1,256]{1,0:T(1,128)S(1)} %bitcast.3, bf16[256,768]{1,0:T(8,128)(2,1)S(1)} %copy-done), custom_call_target="tpu_custom_call" | custom-call | flops 2000000000 | bytes 6000000 | tf_op jit(solution)/shard_map/pallas_call | solution.py:376
  41.2 0.5 collective-permute-done.taken
  41.7 0.2 shard_map.138
  41.9 19.8 %all_to_all.11.back = bf16[16,128,256]{2,1,0:T(8,128)(2,1)S(1)} all-to-all(bf16[16,128,256]{2,1,0:T(8,128)(2,1)S(1)} %shard_map.138), channel_id=1, replica_groups=mesh['dp'=8,'frame'=16] {'frame'}, dimensions={0} | all-to-all | bytes 2097152 | tf_op jit(solution)/shard_map/all_to_all | solution.py:504
  61.7 1.8 %shard_map.139 = (f32[1,1024,256]{2,1,0:T(8,128)}, f32[16,768]{1,0:T(8,128)}, f32[16,256]{1,0:T(8,128)}, f32[16,768]{1,0:T(8,128)}, f32[16,256]{1,0:T(8,128)}, /*index=5*/f32[16]{0:T(128)}, f32[16]{0:T(128)}) custom-call(bf16[16,128,256]{2,1,0:T(8,128)(2,1)S(1)} %all_to_all.11.back, f32[1,256]{1,0:T(1,128)S(1)} %bitcast.4, bf16[256,768]{1,0:T(8,128)(2,1)S(1)} %copy-done, ...), custom_call_target="tpu_custom_call" | custom-call | tf_op jit(solution)/shard_map/pallas_call | solution.py:485
Async XLA Ops:
  2.7 25.6 %copy-start = (bf16[256,768]{1,0:T(8,128)(2,1)S(1)}, bf16[256,768]{1,0:T(8,128)(2,1)}, u32[]{:S(2)}) copy-start(bf16[256,768]{1,0:T(8,128)(2,1)} %weights_t.1) | copy-start | bytes 1179652
  2.8 25.6 %copy-start.1 = (bf16[256,768]{1,0:T(8,128)(2,1)S(1)}, bf16[256,768]{1,0:T(8,128)(2,1)}, u32[]{:S(2)}) copy-start(bf16[256,768]{1,0:T(8,128)(2,1)} %weights_s.1) | copy-start | bytes 1179652
  2.8 25.6 %copy-start.2 = (f32[256]{0:T(256)S(1)}, f32[256]{0:T(256)}, u32[]{:S(2)}) copy-start(f32[256]{0:T(256)} %param.10) | copy-start | bytes 3076
  2.8 25.5 %copy-start.3 = (f32[256]{0:T(256)S(1)}, f32[256]{0:T(256)}, u32[]{:S(2)}) copy-start(f32[256]{0:T(256)} %param.13) | copy-start | bytes 3076
  2.8 25.5 %copy-start.4 = (bf16[256,256]{1,0:T(8,128)(2,1)S(1)}, bf16[256,256]{1,0:T(8,128)(2,1)}, u32[]{:S(2)}) copy-start(bf16[256,256]{1,0:T(8,128)(2,1)} %out_t.1) | copy-start | bytes 393220
  2.8 25.5 %copy-start.5 = (bf16[256,256]{1,0:T(8,128)(2,1)S(1)}, bf16[256,256]{1,0:T(8,128)(2,1)}, u32[]{:S(2)}) copy-start(bf16[256,256]{1,0:T(8,128)(2,1)} %out_s.1) | copy-start | bytes 393220
  38.9 2.8 %collective-permute-start = (bf16[16,64,256]{2,1,0:T(8,128)(2,1)S(1)}, bf16[16,64,256]{2,1,0:T(8,128)(2,1)S(1)}, u32[]{:S(2)}, u32[]{:S(2)}) collective-permute-start(bf16[16,64,256]{2,1,0:T(8,128)(2,1)S(1)} %get-tuple-element.16), channel_id=1, source_target_pairs={{0,1},{1,0},{2,3},{3,2},{4,5},{5,4},{6,7},{7,6},{8,9},{9,8},{10,11... | collective-permute-start | bytes 1572872 | tf_op jit(solution)/shard_map/ppermute | solution.py:513

commit v7 on v6

--- a/solution.py
+++ b/solution.py
@@ -447,7 +447,7 @@
 
 def unpack_kernel(
     back, gains_t, weights_t, gains_s, weights_s,
-    grads, qkv_t, out_t, qkv_s, out_s, gain_t, gain_s, held, sems,
+    grads, qkv_t, out_t, qkv_s, out_s, gain_t, gain_s, held, held_qkv, held_out, sems, weight_sems,
 ):
     copies = []
     for wy in range(4):
@@ -457,10 +457,16 @@
                 for i in range(2):
                     start = 64 * pair + 32 * i + WIN * wx
                     held[wy, start : start + WIN, :] = rows[wx, WIN * i : WIN * (i + 1)]
-        copies.append(
-            pltpu.make_async_copy(held.at[wy], grads.at[0, pl.ds(256 * wy, 256)], sems.at[wy])
-        )
-        copies[wy].start()
+            if pair % 2:
+                first = 64 * (pair - 1)
+                copies.append(
+                    pltpu.make_async_copy(
+                        held.at[wy, pl.ds(first, 128)],
+                        grads.at[0, pl.ds(256 * wy + first, 128)],
+                        sems.at[wy, pair // 2],
+                    )
+                )
+                copies[-1].start()
     inverse = (FRAMES * TOKENS) ** (-0.5)
 
     def total(first, sources):
@@ -473,8 +479,11 @@
     ):
         sources = range(core, FRAMES, 2)
         sums = jnp.concatenate([total(SHARE + 16 * i, sources) for i in range(3)], axis=1)
-        qkv[...] = sums
-        out[...] = total(SHARE + 48, sources)
+        held_qkv[core] = sums
+        held_out[core] = total(SHARE + 48, sources)
+        for n, (src, dst) in enumerate(((held_qkv, qkv), (held_out, out))):
+            copies.append(pltpu.make_async_copy(src.at[core], dst, weight_sems.at[core, n]))
+            copies[-1].start()
         gain_out[...] = gain_sums(sums, weights, gain, me)[0]
     for copy in copies:
         copy.wait()
@@ -485,7 +494,7 @@
     return pl.pallas_call(
         unpack_kernel,
         in_specs=[vmem] * 5,
-        out_specs=[pl.BlockSpec(memory_space=pl.ANY)] + [vmem] * 6,
+        out_specs=[pl.BlockSpec(memory_space=pl.ANY)] * 5 + [vmem] * 2,
         out_shape=(
             shaped(F32, 1, TOKENS, D),
             shaped(F32, 16, 3 * D),
@@ -495,7 +504,13 @@
             shaped(F32, 16),
             shaped(F32, 16),
         ),
-        scratch_shapes=[pltpu.VMEM((4, 256, D), F32), pltpu.SemaphoreType.DMA((4,))],
+        scratch_shapes=[
+            pltpu.VMEM((4, 256, D), F32),
+            pltpu.VMEM((2, 16, 3 * D), F32),
+            pltpu.VMEM((2, 16, D), F32),
+            pltpu.SemaphoreType.DMA((4, 2)),
+            pltpu.SemaphoreType.DMA((2, 2)),
+        ],
         compiler_params=params(8),
     )(back, gain_t, qkv_t, gain_s, qkv_s)
 

time: 63.7 us -> 63.7 us (level)
  no operation moved by 1% of the time
where the time goes in v7:
time: 63.7 us; the launch traced here: 63.4 us
  blocking collectives  45.3 us (71%)
  Pallas kernels  15.6 us (24%)
  starting transfers between devices  1.25 us (2%)
  between operations  0.73 us (1%)
    all_to_all x2, blocking collectives, exchange(): return lax.all_to_all(x, 'frame', split_axis=0, concat_axis=0, tiled=True)  45.3 us
    pallas_call x1, Pallas kernels, run_main(): pl.pallas_call(main_kernel, out_shape=(shaped(BF16, ROWS, D), shaped(BF16...  10.6 us
    pallas_call x1, Pallas kernels, pack(): pl.pallas_call(pack_kernel, in_specs=[anywhere] * 2, out_specs=anywhere,...  2.1 us
    pallas_call x1, Pallas kernels, unpack(): pl.pallas_call(unpack_kernel, in_specs=[vmem] * 5, out_specs=[pl.BlockSpe...  1.73 us
  transfers between devices with their start and end apart: 1, of which 1 were waited for; matrix products, arithmetic and copies ran while one was open for 0% of the time, Pallas kernels for 2%

profile of v7, /device:TPU:1, one launch (start us, length us, event | category | flops | bytes accessed | tf_op | source)
XLA Modules:
  0.0 63.4 jit_solution(1805199455448889309)
XLA Ops:
  0.6 2.1 %shard_map.135 = bf16[16,128,256]{2,1,0:T(8,128)(2,1)} custom-call(bf16[1,1024,256]{2,1,0:T(8,128)(2,1)} %latents.1, bf16[1,1024,256]{2,1,0:T(8,128)(2,1)} %cotangent.1), custom_call_target="tpu_custom_call" | custom-call | tf_op jit(solution)/shard_map/pallas_call | solution.py:425
  2.7 0.0 copy-start
  2.8 0.0 copy-start.1
  2.8 0.0 copy-start.2
  2.8 0.0 copy-start.3
  2.8 0.0 copy-start.4
  2.8 0.0 copy-start.5
  2.8 25.5 %all_to_all.10.moved = bf16[16,128,256]{2,1,0:T(8,128)(2,1)S(1)} all-to-all(bf16[16,128,256]{2,1,0:T(8,128)(2,1)} %shard_map.135), channel_id=1, replica_groups=mesh['dp'=8,'frame'=16] {'frame'}, dimensions={0} | all-to-all | bytes 2097152 | tf_op jit(solution)/shard_map/all_to_all | solution.py:519
  28.3 0.0 copy-done
  28.3 0.0 copy-done.1
  28.3 0.0 copy-done.2
  28.3 0.0 copy-done.3
  28.3 0.0 copy-done.4
  28.3 0.0 copy-done.5
  28.4 10.6 %shard_map.136 = (bf16[1024,256]{1,0:T(8,128)(2,1)S(1)}, bf16[1024,768]{1,0:T(8,128)(2,1)S(1)}, f32[16,64,256]{2,1,0:T(8,128)S(1)}, bf16[16,64,256]{2,1,0:T(8,128)(2,1)S(1)}, bf16[16,64,256]{2,1,0:T(8,128)(2,1)S(1)}) custom-call(bf16[16,128,256]{2,1,0:T(8,128)(2,1)S(1)} %all_to_all.10.moved, f32[1,256]{1,0:T(1,128)S(1)} %bitcast.2, ...), custom_call_target="tpu_custom_call" | custom-call | flops 8000000000 | bytes 6000000 | tf_op jit(solution)/shard_map/pallas_call | solution.py:344
  38.9 1.2 %collective-permute-start = (bf16[16,64,256]{2,1,0:T(8,128)(2,1)S(1)}, bf16[16,64,256]{2,1,0:T(8,128)(2,1)S(1)}, u32[]{:S(2)}, u32[]{:S(2)}) collective-permute-start(bf16[16,64,256]{2,1,0:T(8,128)(2,1)S(1)} %get-tuple-element.16), channel_id=1, source_target_pairs={{0,1},{1,0},{2,3},{3,2},{4,5},{5,4},{6,7},{7,6},{8,9},{9,8},{10,11... | collective-permute-start | bytes 1572872 | tf_op jit(solution)/shard_map/ppermute | solution.py:528
  40.2 1.0 %shard_map.137.grads = bf16[16,64,256]{2,1,0:T(8,128)(2,1)S(1)} custom-call(bf16[1024,256]{1,0:T(8,128)(2,1)S(1)} %get-tuple-element.12.xs, bf16[1024,768]{1,0:T(8,128)(2,1)S(1)} %get-tuple-element.13.dproj, f32[16,64,256]{2,1,0:T(8,128)S(1)} %get-tuple-element.14.dmid, f32[1,256]{1,0:T(1,128)S(1)} %bitcast.3, bf16[256,768]{1,0:T(8,128)(2,1)S(1)} %copy-done), custom_call_target="tpu_custom_call" | custom-call | flops 2000000000 | bytes 6000000 | tf_op jit(solution)/shard_map/pallas_call | solution.py:376
  41.2 0.5 collective-permute-done.taken
  41.7 0.2 shard_map.138
  41.9 19.8 %all_to_all.11.back = bf16[16,128,256]{2,1,0:T(8,128)(2,1)S(1)} all-to-all(bf16[16,128,256]{2,1,0:T(8,128)(2,1)S(1)} %shard_map.138), channel_id=1, replica_groups=mesh['dp'=8,'frame'=16] {'frame'}, dimensions={0} | all-to-all | bytes 2097152 | tf_op jit(solution)/shard_map/all_to_all | solution.py:519
  61.7 1.7 %shard_map.139 = (f32[1,1024,256]{2,1,0:T(8,128)}, f32[16,768]{1,0:T(8,128)}, f32[16,256]{1,0:T(8,128)}, f32[16,768]{1,0:T(8,128)}, f32[16,256]{1,0:T(8,128)}, /*index=5*/f32[16]{0:T(128)}, f32[16]{0:T(128)}) custom-call(bf16[16,128,256]{2,1,0:T(8,128)(2,1)S(1)} %all_to_all.11.back, f32[1,256]{1,0:T(1,128)S(1)} %bitcast.4, bf16[256,768]{1,0:T(8,128)(2,1)S(1)} %copy-done, ...), custom_call_target="tpu_custom_call" | custom-call | tf_op jit(solution)/shard_map/pallas_call | solution.py:494
Async XLA Ops:
  2.7 25.6 %copy-start = (bf16[256,768]{1,0:T(8,128)(2,1)S(1)}, bf16[256,768]{1,0:T(8,128)(2,1)}, u32[]{:S(2)}) copy-start(bf16[256,768]{1,0:T(8,128)(2,1)} %weights_t.1) | copy-start | bytes 1179652
  2.8 25.6 %copy-start.1 = (bf16[256,768]{1,0:T(8,128)(2,1)S(1)}, bf16[256,768]{1,0:T(8,128)(2,1)}, u32[]{:S(2)}) copy-start(bf16[256,768]{1,0:T(8,128)(2,1)} %weights_s.1) | copy-start | bytes 1179652
  2.8 25.6 %copy-start.2 = (f32[256]{0:T(256)S(1)}, f32[256]{0:T(256)}, u32[]{:S(2)}) copy-start(f32[256]{0:T(256)} %param.10) | copy-start | bytes 3076
  2.8 25.5 %copy-start.3 = (f32[256]{0:T(256)S(1)}, f32[256]{0:T(256)}, u32[]{:S(2)}) copy-start(f32[256]{0:T(256)} %param.13) | copy-start | bytes 3076
  2.8 25.5 %copy-start.4 = (bf16[256,256]{1,0:T(8,128)(2,1)S(1)}, bf16[256,256]{1,0:T(8,128)(2,1)}, u32[]{:S(2)}) copy-start(bf16[256,256]{1,0:T(8,128)(2,1)} %out_t.1) | copy-start | bytes 393220
  2.8 25.5 %copy-start.5 = (bf16[256,256]{1,0:T(8,128)(2,1)S(1)}, bf16[256,256]{1,0:T(8,128)(2,1)}, u32[]{:S(2)}) copy-start(bf16[256,256]{1,0:T(8,128)(2,1)} %out_s.1) | copy-start | bytes 393220
  38.9 2.8 %collective-permute-start = (bf16[16,64,256]{2,1,0:T(8,128)(2,1)S(1)}, bf16[16,64,256]{2,1,0:T(8,128)(2,1)S(1)}, u32[]{:S(2)}, u32[]{:S(2)}) collective-permute-start(bf16[16,64,256]{2,1,0:T(8,128)(2,1)S(1)} %get-tuple-element.16), channel_id=1, source_target_pairs={{0,1},{1,0},{2,3},{3,2},{4,5},{5,4},{6,7},{7,6},{8,9},{9,8},{10,11... | collective-permute-start | bytes 1572872 | tf_op jit(solution)/shard_map/ppermute | solution.py:528
